TPU v7x, 32 devices: a whole 2x2x4 slice. The times are simulated.
32 devices in a mesh: seq: 8 (over z, x), dp: 4 (over y, core).
Axes of the slice: x: 2, y: 2, z: 4, core: 2. Of those that a mesh axis runs over, the one named last changes fastest.
Arguments:
- x_in: bfloat16 [4, 2048, 2048], P('dp', 'seq'), may hold values from -6 to 6
- gate_in: bfloat16 [4, 2048, 2048], P('dp', 'seq'), may hold values from -6 to 6
- keys_b: bfloat16 [4, 2048, 128], P('dp', 'seq'), may hold values from -6 to 6
- queries_c: bfloat16 [4, 2048, 128], P('dp', 'seq'), may hold values from -0.5 to 0.5
- decay_log: float32 [4, 32, 2048], P('dp', None, 'seq'), may hold values from -0.8 to 0
- level_mix: float32 [4, 12, 32, 2048], P('dp', None, None, 'seq'), may hold values from 0.2 to 2
- norm_gain: float32 [2048], replicated, may hold values from 0.25 to 1.75
- w_gate: bfloat16 [2048, 2816], P(None, ('seq', 'dp')), may hold values from -0.125 to 0.125
- w_up: bfloat16 [2048, 2816], P(None, ('seq', 'dp')), may hold values from -0.125 to 0.125
Outputs:
- hidden: bfloat16 [4, 2048, 2816], P('dp', 'seq')
All inputs are finite; a program needn't handle non-finite values.
Results may differ from a plain program's by a relative error of at most 0.0078.
Values may be sent and summed in bfloat16 or wider, within the bound.
A program may use at most 128 MiB of HBM per device.

v0:
```python
import jax
import jax.numpy as jnp
from jax import lax
from jax.sharding import PartitionSpec as P

SPAN = 256
SPAN_BITS = 8


EPS = 1e-05
HIGH = lax.Precision.HIGHEST


def swapped(value, axis, distance):
    mask = 2**distance
    pairs = [(source, source ^ mask) for source in range(lax.axis_size(axis))]
    return lax.ppermute(value, axis, pairs)


def top_bit(values):
    powers = jnp.arange(1, 31, dtype=jnp.int32)
    return jnp.sum(values[..., None] >> powers > 0, axis=-1)


def block_inner(x_blk, b_blk, c_blk, a_blk, mix_low):
    length = a_blk.shape[1]
    inner_count = mix_low.shape[0]
    running = jnp.cumsum(a_blk, axis=1)
    position = jnp.arange(length, dtype=jnp.int32)
    differ = position[:, None] ^ position[None, :]
    level_table = jnp.where(differ > 0, top_bit(differ) + 1, 0)
    level_picks = (
        level_table[None] == jnp.arange(inner_count, dtype=jnp.int32)[:, None, None]
    ).astype(jnp.float32)
    chosen = jnp.einsum("lht,lts->hts", mix_low, level_picks, precision=HIGH)
    causal_mask = position[:, None] >= position[None, :]
    log_gap = jnp.where(causal_mask[None], running[:, :, None] - running[:, None, :], -jnp.inf)
    scores = jnp.dot(c_blk, b_blk.T, preferred_element_type=jnp.float32)
    weights = (chosen * jnp.exp(log_gap) * scores[None]).astype(jnp.bfloat16)
    local_part = jnp.einsum("hts,shp->thp", weights, x_blk, preferred_element_type=jnp.float32)
    tail_decay = jnp.exp(running[:, -1:] - running)
    scaled_keys = (tail_decay.T[:, :, None] * b_blk[:, None, :]).astype(jnp.bfloat16)
    block_state = jnp.einsum("shn,shp->hnp", scaled_keys, x_blk, preferred_element_type=jnp.float32)
    return (local_part, block_state, running)


def block_distant(c_blk, running, mix_high, levels):
    growth = jnp.exp(running)
    distant_sum = jnp.zeros((c_blk.shape[0], running.shape[0], levels[0].shape[2]), jnp.float32)
    for level_rank in range(len(levels)):
        level_scale = (mix_high[level_rank] * growth).T
        product = jnp.einsum(
            "tn,hnp->thp",
            c_blk,
            levels[level_rank].astype(jnp.bfloat16),
            preferred_element_type=jnp.float32,
        )
        distant_sum = distant_sum + level_scale[:, :, None] * product
    return distant_sum


def per_device(x_in, gate_in, keys_b, queries_c, decay_log, level_mix, norm_gain, w_gate, w_up):
    tok_dev = x_in.shape[1]
    embedding_width = x_in.shape[2]
    head_count = decay_log.shape[1]
    head_dim = embedding_width // head_count
    blocks = tok_dev // SPAN
    inner_count = SPAN_BITS + 1
    seq_bits = lax.axis_size("seq").bit_length() - 1
    x_blocks = x_in[0].reshape(blocks, SPAN, head_count, head_dim)
    b_blocks = keys_b[0].reshape(blocks, SPAN, -1)
    c_blocks = queries_c[0].reshape(blocks, SPAN, -1)
    a_blocks = decay_log[0].reshape(head_count, blocks, SPAN)
    mix_all = level_mix[0].reshape(level_mix.shape[1], head_count, blocks, SPAN)
    local_parts, block_states, block_decays, runnings = ([], [], [], [])
    block_index = 0
    local_part, block_state, running = block_inner(
        x_blocks[block_index],
        b_blocks[block_index],
        c_blocks[block_index],
        a_blocks[:, block_index],
        mix_all[:inner_count, :, block_index],
    )
    local_parts.append(local_part)
    block_states.append(block_state)
    block_decays.append(running[:, -1])
    runnings.append(running)
    summary = jnp.zeros_like(block_states[0])
    block_index = 0
    summary = (
        jnp.exp(block_decays[block_index])[:, None, None] * summary + block_states[block_index]
    )
    summary_decay = block_decays[block_index]
    rank_here = lax.axis_index("seq")
    own_prefix = jnp.zeros((head_count,), jnp.float32)
    device_levels = []
    for bit_index in range(seq_bits):
        other_state, other_decay = swapped((summary, summary_decay), "seq", bit_index)
        is_upper = rank_here >> bit_index & 1 == 1
        device_levels.append(
            jnp.where(is_upper, jnp.exp(own_prefix)[:, None, None] * other_state, 0.0)
        )
        lower_state = jnp.where(is_upper, other_state, summary)
        lower_decay = jnp.where(is_upper, other_decay, summary_decay)
        upper_state = jnp.where(is_upper, summary, other_state)
        upper_decay = jnp.where(is_upper, summary_decay, other_decay)
        summary = jnp.exp(upper_decay)[:, None, None] * lower_state + upper_state
        summary_decay = lower_decay + upper_decay
        own_prefix = jnp.where(is_upper, own_prefix + other_decay, own_prefix)
    zero_decay = jnp.zeros((head_count,), jnp.float32)
    block_index = 0
    levels = []
    lead_decay = sum(block_decays[:block_index], zero_decay)
    for device_level in device_levels:
        levels.append(jnp.exp(lead_decay)[:, None, None] * device_level)
    distant = block_distant(
        c_blocks[block_index], runnings[block_index], mix_all[inner_count:, :, block_index], levels
    )
    outputs = local_parts[block_index] + distant
    mixed = outputs.reshape(tok_dev, embedding_width)
    gated = mixed * jax.nn.silu(gate_in[0].astype(jnp.float32))
    normed = (
        gated * lax.rsqrt(jnp.mean(gated * gated, axis=-1, keepdims=True) + EPS) * norm_gain
    ).astype(jnp.bfloat16)
    paired = jnp.stack([w_gate, w_up])
    dp_count = lax.axis_size("dp")
    seq_count = lax.axis_size("seq")
    seq_weights = lax.all_gather(paired, "seq", axis=2, tiled=True)
    projected = jnp.einsum(
        "td,gdk->gtk",
        normed,
        lax.all_gather(seq_weights, "dp", axis=2, tiled=True),
        preferred_element_type=jnp.float32,
    )
    returned = (jax.nn.silu(projected[0]) * projected[1]).astype(jnp.bfloat16)
    hidden = (
        returned.reshape(tok_dev, dp_count, seq_count, -1)
        .transpose(0, 2, 1, 3)
        .reshape(tok_dev, -1)
    )
    return hidden[None]


def solution(mesh):
    in_specs = (
        P("dp", "seq", None),
        P("dp", "seq", None),
        P("dp", "seq", None),
        P("dp", "seq", None),
        P("dp", None, "seq"),
        P("dp", None, None, "seq"),
        P(),
        P(None, ("seq", "dp")),
        P(None, ("seq", "dp")),
    )
    out_specs = P("dp", "seq", None)
    return jax.shard_map(
        per_device, mesh=mesh, in_specs=in_specs, out_specs=out_specs, check_vma=False
    )
```

profile of v0, /device:TPU:0, one launch (start us, length us, event | category | flops | bytes accessed | tf_op | source)
XLA Modules:
  0.0 268.6 jit_solution(4944152109733875630)
XLA Ops:
  6.5 0.0 all-gather.3.cloned.1.call-start
  6.5 2.0 pad_maximum_fusion
  8.6 0.0 all-gather.3.cloned.1.call-update
  8.6 0.0 all-gather.5.cloned.1.call-start
  8.7 96.3 %all-gather.3.cloned.1.call-done = bf16[2,2048,704]{1,2,0:T(8,128)(2,1)} async-done(((bf16[2,2048,88]{1,2,0:T(8,128)(2,1)}), bf16[2,2048,704]{1,2,0:T(8,128)(2,1)}) %all-gather.3.cloned.1.call-update) | async-done | bytes 5767184 | tf_op jit(solution)/shard_map/all_gather | solution.py:128
  104.9 0.0 all-gather.5.cloned.1.call-update
  105.0 0.7 copy-done.12
  105.7 0.6 reduce-window.6
  106.3 0.2 slice_reduce_fusion
  106.5 0.1 copy_bitcast_fusion
  106.6 0.2 slice_reduce_fusion.1
  106.8 0.6 collective-permute-start.1
  107.4 0.0 copy-done.4
  107.4 0.7 fusion.45
  108.1 0.5 copy.29
  108.7 1.7 collective-permute-done.1
  110.4 2.4 fusion.21
  112.9 0.6 collective-permute-start
  113.4 0.7 copy.28
  114.1 0.6 iota_compare_fusion.4
  114.8 21.3 %collective-permute-done = f32[32,128,64]{1,2,0:T(8,128)S(1)} collective-permute-done((f32[32,128,64]{1,2,0:T(8,128)}, f32[32,128,64]{1,2,0:T(8,128)S(1)}, u32[]{:S(2)}, u32[]{:S(2)}) %collective-permute-start) | collective-permute-done | bytes 1048608 | tf_op jit(solution)/shard_map/ppermute | solution.py:17
  136.1 2.5 select_add_fusion.1
  138.6 0.0 collective-permute-start.2
  138.6 1.7 fusion.40
  140.3 1.1 convert_reduce_fusion
  141.4 0.7 add_select_fusion
  142.2 2.0 collective-permute-start.3
  144.2 2.5 copy.37
  146.7 14.4 %collective-permute-done.3 = f32[32]{0:T(128)S(1)} collective-permute-done((f32[32]{0:T(128)S(1)}, f32[32]{0:T(128)S(1)}, u32[]{:S(2)}, u32[]{:S(2)}) %collective-permute-start.3) | collective-permute-done | bytes 160 | tf_op jit(solution)/shard_map/ppermute | solution.py:17
  161.1 0.0 collective-permute-done.2
  161.1 2.4 select_add_fusion
  163.5 2.1 collective-permute-start.4
  165.6 7.5 %fusion.1 = bf16[32,256,256]{2,0,1:T(8,128)(2,1)} fusion(f32[256,256]{1,0:T(8,128)S(1)} %copy-done.7, f32[32,256]{1,0:T(8,128)S(1)} %copy_bitcast_fusion, f32[32,256]{0,1:T(8,128)S(1)} %copy-done.10, pred[256,256]{1,0:T(8,128)(4,1)S(1)} %copy-done.11, f32[1,9,32,256]{2,1,3,0:T(8,128)S(1)} %copy-done.2, s32[256,256]{1,0:T(8,128)S(1)} %copy-done.8), kind=kOutput, calls=%fused_computation.2 | convolution fusion | flops 237568000 | bytes 5144576 | tf_op jit(solution)/shard_map/lht,lts->hts/dot_general | solution.py:35
  173.1 2.5 copy.32
  175.7 4.7 %fusion.2 = f32[32,256,64]{1,2,0:T(8,128)S(1)} fusion(bf16[256,32,64]{0,2,1:T(8,128)(2,1)S(1)} %bitcast.121, bf16[32,256,256]{2,0,1:T(8,128)(2,1)} %fusion.1), kind=kOutput, calls=%fused_computation.6 | convolution fusion | flops 268435456 | bytes 7340032 | tf_op jit(solution)/shard_map/hts,shp->thp/dot_general | solution.py:40
  180.3 0.4 fusion.26
  180.8 0.0 copy-start.3
  180.8 0.5 fusion.27
  181.3 27.3 %collective-permute-done.4 = f32[32,128,64]{1,2,0:T(8,128)} collective-permute-done((f32[32,128,64]{1,2,0:T(8,128)}, f32[32,128,64]{1,2,0:T(8,128)}, u32[]{:S(2)}, u32[]{:S(2)}) %collective-permute-start.4) | collective-permute-done | bytes 1048608 | tf_op jit(solution)/shard_map/ppermute | solution.py:17
  208.6 2.5 multiply_reduce_fusion
  211.1 0.0 copy-start.16
  211.2 1.9 copy.31
  213.0 33.6 %all-gather.5.cloned.1.call-done = bf16[2,2048,2816]{1,2,0:T(8,128)(2,1)} async-done(((bf16[2,2048,704]{1,2,0:T(8,128)(2,1)}), bf16[2,2048,2816]{1,2,0:T(8,128)(2,1)}) %all-gather.5.cloned.1.call-update) | async-done | bytes 23068688 | tf_op jit(solution)/shard_map/all_gather | solution.py:132
  246.6 12.2 %convolution_bitcast_fusion = f32[2,256,2816]{1,2,0:T(8,128)S(1)} fusion(bf16[2,2048,2816]{1,2,0:T(8,128)(2,1)} %all-gather.5.cloned.1.call-done, f32[256,2048]{1,0:T(8,128)} %copy.31, f32[2048]{0:T(1024)S(1)} %copy-done.16, f32[256]{0:T(256)S(1)} %add_rsqrt_fusion, bf16[1,256,2048]{2,1,0:T(8,128)(2,1)S(1)} %copy-done.5), kind=kOutput, calls=%fused_computation.5 | convolution fusion | flops 5910298624 | bytes 31990784 | tf_op jit(solution)/shard_map/td,gdk->gtk/dot_general | solution.py:129
  258.8 0.4 fusion.55
  259.2 0.0 copy-start.1
  259.2 0.8 fusion.5
  260.0 1.7 copy.36
  (41 shorter events, 0.2 us)
Async XLA Ops:
  6.5 132.1 %copy-start = (bf16[1,256,128]{2,1,0:T(8,128)(2,1)S(1)}, bf16[1,256,128]{2,1,0:T(8,128)(2,1)}, u32[]{:S(2)}) copy-start(bf16[1,256,128]{2,1,0:T(8,128)(2,1)} %param.12) | copy-start | bytes 196612
  6.5 98.4 %all-gather.3.cloned.1.call-start = ((), (), s32[]{:S(2)}) async-start(), calls=%async_computation | async-start | bytes 6488064 | tf_op jit(solution)/shard_map/all_gather | solution.py:128
  8.6 238.0 %all-gather.5.cloned.1.call-start = ((), (), s32[]{:S(2)}) async-start(), calls=%async_computation.1 | async-start | bytes 28835840 | tf_op jit(solution)/shard_map/all_gather | solution.py:132
  104.9 0.8 copy-start.12
  104.9 2.5 copy-start.9
  104.9 2.5 copy-start.4
  104.9 3.2 %copy-start.6 = (bf16[1,256,2048]{2,1,0:T(8,128)(2,1)S(1)}, bf16[1,256,2048]{2,1,0:T(8,128)(2,1)}, u32[]{:S(2)}) copy-start(bf16[1,256,2048]{2,1,0:T(8,128)(2,1)} %param.9) | copy-start | bytes 3145732
  106.8 3.6 %collective-permute-start.1 = (f32[32]{0:T(128)S(1)}, f32[32]{0:T(128)S(1)}, u32[]{:S(2)}, u32[]{:S(2)}) collective-permute-start(f32[32]{0:T(128)S(1)} %slice_reduce_fusion.1), channel_id=1, source_target_pairs={{0,4},{4,0},{8,12},{12,8},{16,20},{20,16},{24,28},{28,24},{1,5},{5... | collective-permute-start | bytes 392 | tf_op jit(solution)/shard_map/ppermute | solution.py:17
  112.9 23.3 %collective-permute-start = (f32[32,128,64]{1,2,0:T(8,128)}, f32[32,128,64]{1,2,0:T(8,128)S(1)}, u32[]{:S(2)}, u32[]{:S(2)}) collective-permute-start(f32[32,128,64]{1,2,0:T(8,128)} %fusion.21), channel_id=1, source_target_pairs={{0,4},{4,0},{8,12},{12,8},{16,20},{20,16},{24,28},{28,24},{1,5},{5... | collective-permute-start | bytes 3145736 | tf_op jit(solution)/shard_map/ppermute | solution.py:17
  136.1 8.1 %slice-start = ((f32[1,12,32,256]{3,2,1,0:T(8,128)}), f32[1,9,32,256]{3,2,1,0:T(8,128)S(1)}, s32[]{:S(2)}) async-start(f32[1,12,32,256]{3,2,1,0:T(8,128)} %param.14), calls=%async_computation.2 | async-start | bytes 589824 | tf_op jit(solution)/shard_map/slice | solution.py:82
  138.6 22.5 %collective-permute-start.2 = (f32[32,128,64]{1,2,0:T(8,128)}, f32[32,128,64]{1,2,0:T(8,128)S(1)}, u32[]{:S(2)}, u32[]{:S(2)}) collective-permute-start(f32[32,128,64]{1,2,0:T(8,128)} %select_add_fusion.1), channel_id=1, source_target_pairs={{0,8},{4,12},{8,0},{12,4},{16,24},{20,28},{24,16},{28,20},{1,9},{5... | collective-permute-start | bytes 3145736 | tf_op jit(solution)/shard_map/ppermute | solution.py:17
  142.2 18.9 %collective-permute-start.3 = (f32[32]{0:T(128)S(1)}, f32[32]{0:T(128)S(1)}, u32[]{:S(2)}, u32[]{:S(2)}) collective-permute-start(f32[32]{0:T(128)S(1)} %get-tuple-element.11), channel_id=1, source_target_pairs={{0,8},{4,12},{8,0},{12,4},{16,24},{20,28},{24,16},{28,20},{1,9},{5... | collective-permute-start | bytes 392 | tf_op jit(solution)/shard_map/ppermute | solution.py:17
  146.7 18.9 %copy-start.2 = (f32[1,9,32,256]{2,1,3,0:T(8,128)S(1)}, f32[1,9,32,256]{2,1,3,0:T(8,128)}, u32[]{:S(2)}) copy-start(f32[1,9,32,256]{2,1,3,0:T(8,128)} %copy.37) | copy-start | bytes 884740
  146.7 18.9 %copy-start.7 = (f32[256,256]{1,0:T(8,128)S(1)}, f32[256,256]{1,0:T(8,128)}, u32[]{:S(2)}) copy-start(f32[256,256]{1,0:T(8,128)} %fusion.40) | copy-start | bytes 786436
  146.7 18.9 %copy-start.8 = (s32[256,256]{1,0:T(8,128)S(1)}, s32[256,256]{1,0:T(8,128)}, u32[]{:S(2)}) copy-start(s32[256,256]{1,0:T(8,128)} %add_select_fusion) | copy-start | bytes 786436
  146.7 18.9 %copy-start.10 = (f32[32,256]{0,1:T(8,128)S(1)}, f32[32,256]{0,1:T(8,128)}, u32[]{:S(2)}) copy-start(f32[32,256]{0,1:T(8,128)} %copy.28) | copy-start | bytes 98308
  146.7 18.9 %copy-start.11 = (pred[256,256]{1,0:T(8,128)(4,1)S(1)}, pred[256,256]{1,0:T(8,128)(4,1)}, u32[]{:S(2)}) copy-start(pred[256,256]{1,0:T(8,128)(4,1)} %iota_compare_fusion.4) | copy-start | bytes 196612
  163.5 45.0 %collective-permute-start.4 = (f32[32,128,64]{1,2,0:T(8,128)}, f32[32,128,64]{1,2,0:T(8,128)}, u32[]{:S(2)}, u32[]{:S(2)}) collective-permute-start(f32[32,128,64]{1,2,0:T(8,128)} %select_add_fusion), channel_id=1, source_target_pairs={{0,16},{4,20},{8,24},{12,28},{16,0},{20,4},{24,8},{28,12},{1,17},{... | collective-permute-start | bytes 3145736 | tf_op jit(solution)/shard_map/ppermute | solution.py:17
  180.8 27.8 %copy-start.3 = (f32[1,256,2048]{1,2,0:T(8,128)S(1)}, f32[1,256,2048]{1,2,0:T(8,128)}, u32[]{:S(2)}) copy-start(f32[1,256,2048]{1,2,0:T(8,128)} %copy.32) | copy-start | bytes 6291460
  180.8 27.8 %copy-start.13 = (f32[256,32]{0,1:T(8,128)S(1)}, f32[256,32]{0,1:T(8,128)}, u32[]{:S(2)}) copy-start(f32[256,32]{0,1:T(8,128)} %get-tuple-element.7) | copy-start | bytes 98308
  180.8 27.8 %copy-start.14 = (f32[256,32]{0,1:T(8,128)S(1)}, f32[256,32]{0,1:T(8,128)}, u32[]{:S(2)}) copy-start(f32[256,32]{0,1:T(8,128)} %get-tuple-element.8) | copy-start | bytes 98308
  180.8 27.8 %copy-start.15 = (f32[256,32]{0,1:T(8,128)S(1)}, f32[256,32]{0,1:T(8,128)}, u32[]{:S(2)}) copy-start(f32[256,32]{0,1:T(8,128)} %get-tuple-element.9) | copy-start | bytes 98308
  211.1 35.5 %copy-start.5 = (bf16[1,256,2048]{2,1,0:T(8,128)(2,1)S(1)}, bf16[1,256,2048]{2,1,0:T(8,128)(2,1)}, u32[]{:S(2)}) copy-start(bf16[1,256,2048]{2,1,0:T(8,128)(2,1)} %param.10) | copy-start | bytes 3145732
  211.1 35.5 %copy-start.16 = (f32[2048]{0:T(1024)S(1)}, f32[2048]{0:T(1024)}, u32[]{:S(2)}) copy-start(f32[2048]{0:T(1024)} %param.15) | copy-start | bytes 24580
  259.2 2.5 copy-start.1
Sparse Core Ops, SparseCore 0:
  9.6 95.3 all-gather.2
  106.5 140.0 all-gather.4
where the time goes:
time: 269 us
  waiting for transfers between devices  195 us (72%)
  matrix products  32 us (12%)
  between operations  13.6 us (5%)
  other arithmetic  11.7 us (4%)
  local copies, waits for them, and re-layouts  11.4 us (4%)
  starting transfers between devices  5.3 us (2%)
    all_gather x1, waiting for transfers between devices, per_device(): seq_weights = lax.all_gather(paired, 'seq', axis=2, tiled=True)  96.3 us
    ppermute x5, waiting for transfers between devices, swapped(): return lax.ppermute(value, axis, pairs)  64.7 us
    all_gather x1, waiting for transfers between devices, per_device(): lax.all_gather(seq_weights, 'dp', axis=2, tiled=True)  33.6 us
    dot_general x1, matrix products, per_device(): jnp.einsum('td,gdk->gtk', normed, lax.all_gather(seq_weights, 'dp', axis=...  12.2 us
    dot_general x1, matrix products, block_inner(): chosen = jnp.einsum('lht,lts->hts', mix_low, level_picks, precision=HIGH)  7.48 us
  transfers between devices with their start and end apart: 7, of which 6 were waited for; matrix products, arithmetic and copies ran while one was open for 14% of the time, Pallas kernels for 0%

commit v1 on v0

--- a/solution.py
+++ b/solution.py
@@ -1,6 +1,8 @@
 import jax
 import jax.numpy as jnp
 from jax import lax
+from jax.experimental import pallas as pl
+from jax.experimental.pallas import tpu as pltpu
 from jax.sharding import PartitionSpec as P
 
 SPAN = 256
@@ -57,6 +59,205 @@
         )
         distant_sum = distant_sum + level_scale[:, :, None] * product
     return distant_sum
+
+
+def gathered_projection(normed, w_gate, w_up):
+    tok_dev = normed.shape[0]
+    paired = jnp.stack([w_gate, w_up])
+    dp_count = lax.axis_size("dp")
+    seq_count = lax.axis_size("seq")
+    seq_weights = lax.all_gather(paired, "seq", axis=2, tiled=True)
+    projected = jnp.einsum(
+        "td,gdk->gtk",
+        normed,
+        lax.all_gather(seq_weights, "dp", axis=2, tiled=True),
+        preferred_element_type=jnp.float32,
+    )
+    returned = (jax.nn.silu(projected[0]) * projected[1]).astype(jnp.bfloat16)
+    hidden = (
+        returned.reshape(tok_dev, dp_count, seq_count, -1)
+        .transpose(0, 2, 1, 3)
+        .reshape(tok_dev, -1)
+    )
+    return hidden
+
+
+MESH = pl.DeviceIdType.MESH
+SEQ_COUNT = 8
+DP_COUNT = 4
+LINE = 4
+CHIPS = 16
+
+
+def line_member(z, steps):
+    place = z + (z >= 2) * (5 - 2 * z)
+    back = lax.rem(place - steps + 2 * LINE, LINE)
+    return back + (back >= 2) * (5 - 2 * back)
+
+
+class Gather:
+    def __init__(self, piece, held, z_sems, x_sems, y_sems, core_sems, own_sem):
+        self.piece, self.held, self.own_sem = piece, held, own_sem
+        self.sems = {"z": z_sems, "x": x_sems, "y": y_sems, "core": core_sems}
+        seq, dp = lax.axis_index("seq"), lax.axis_index("dp")
+        self.z, self.x, self.y, self.core = seq // 2, lax.rem(seq, 2), dp // 2, lax.rem(dp, 2)
+        self.targets = {
+            "z": (line_member(self.z, -1) * 2 + self.x, dp),
+            "x": (self.z * 2 + 1 - self.x, dp),
+            "y": (seq, (1 - self.y) * 2 + self.core),
+            "core": (seq, self.y * 2 + 1 - self.core),
+        }
+        self.before = (line_member(self.z, 1) * 2 + self.x, dp)
+        self.sent = []
+
+    def greet(self):
+        barrier = pltpu.get_barrier_semaphore()
+        others = list(self.targets.values()) + [self.before]
+        for other in others:
+            pl.semaphore_signal(barrier, inc=1, device_id=other, device_id_type=MESH)
+        pl.semaphore_wait(barrier, len(others))
+
+    def chip(self, step, flip_x, flip_y):
+        x = 1 - self.x if flip_x else self.x
+        y = 1 - self.y if flip_y else self.y
+        return line_member(self.z, step) * 4 + x * 2 + y
+
+    def copy(self, way, slot, chip, own=False):
+        place = self.held.at[self.core, chip]
+        return pltpu.make_async_remote_copy(
+            src_ref=self.piece if own else place,
+            dst_ref=place,
+            send_sem=self.sems[way].at[0, slot],
+            recv_sem=self.sems[way].at[1, slot],
+            device_id=self.targets[way],
+            device_id_type=MESH,
+        )
+
+    def send(self, way, slot, chip, own=False):
+        copy = self.copy(way, slot, chip, own)
+        copy.start()
+        self.sent.append(copy)
+
+    def start(self):
+        chip = self.chip(0, 0, 0)
+        self.own = pltpu.make_async_copy(self.piece, self.held.at[self.core, chip], self.own_sem)
+        self.own.start()
+        for way in ("z", "x", "y", "core"):
+            self.send(way, 0, chip, own=True)
+
+    def line(self, step):
+        chip = self.chip(step, 0, 0)
+        self.copy("z", step - 1, chip).wait_recv()
+        if step < LINE - 1:
+            self.send("z", step, chip)
+        for way in ("x", "y"):
+            self.send(way, step, chip)
+        self.send("core", step * 4, chip)
+
+    def across_x(self, step):
+        chip = self.chip(step, 1, 0)
+        self.copy("x", step, chip).wait_recv()
+        if step < 2:
+            self.send("y", LINE + step, chip)
+        self.send("core", step * 4 + 1, chip)
+
+    def across_y(self, step):
+        chip = self.chip(step, 0, 1)
+        self.copy("y", step, chip).wait_recv()
+        if step >= 2:
+            self.send("x", LINE + step - 2, chip)
+        self.send("core", step * 4 + 2, chip)
+
+    def corner(self, step):
+        chip = self.chip(step, 1, 1)
+        way = "y" if step < 2 else "x"
+        self.copy(way, LINE + step % 2, chip).wait_recv()
+        self.send("core", step * 4 + 3, chip)
+
+    def ready(self, step, kind):
+        chip = self.chip(step, kind % 2, kind // 2)
+        place = self.held.at[1 - self.core, chip]
+        pltpu.make_async_remote_copy(
+            src_ref=place,
+            dst_ref=place,
+            send_sem=self.sems["core"].at[0, step * 4 + kind],
+            recv_sem=self.sems["core"].at[1, step * 4 + kind],
+            device_id=self.targets["core"],
+            device_id_type=MESH,
+        ).wait_recv()
+        return chip
+
+    def finish(self):
+        for copy in self.sent:
+            copy.wait_send()
+
+
+def project(normed, held, hidden, chip):
+    contract = (((1,), (1,)), ((), ()))
+    gate = lax.dot_general(normed[...], held[0, chip], contract, preferred_element_type=jnp.float32)
+    up = lax.dot_general(normed[...], held[1, chip], contract, preferred_element_type=jnp.float32)
+    hidden[chip] = (gate / (1.0 + jnp.exp(-gate)) * up).astype(hidden.dtype)
+
+
+def projection_kernel(normed, piece, hidden, held, z_sems, x_sems, y_sems, core_sems, own_sem):
+    gather = Gather(piece, held, z_sems, x_sems, y_sems, core_sems, own_sem)
+    gather.greet()
+    gather.start()
+    gather.own.wait()
+    project(normed, held, hidden, gather.ready(0, 0))
+    for step in range(LINE):
+        gather.across_x(step)
+        gather.across_y(step)
+        if step + 1 < LINE:
+            gather.line(step + 1)
+        project(normed, held, hidden, gather.ready(step, 1))
+        project(normed, held, hidden, gather.ready(step, 2))
+        if step >= 1:
+            gather.corner(step - 1)
+            project(normed, held, hidden, gather.ready(step - 1, 3))
+        if step + 1 < LINE:
+            project(normed, held, hidden, gather.ready(step + 1, 0))
+    gather.corner(LINE - 1)
+    project(normed, held, hidden, gather.ready(LINE - 1, 3))
+    gather.finish()
+
+
+def chip_rows(w_gate, w_up):
+    first = lax.axis_index("dp") % 2 == 0
+    gate, up = w_gate.T, w_up.T
+    pairs = [(source, source ^ 1) for source in range(DP_COUNT)]
+    other = lax.ppermute(jnp.where(first, up, gate), "dp", pairs)
+    return jnp.where(first, jnp.concatenate([gate, other]), jnp.concatenate([other, up]))
+
+
+def streamed_projection(normed, w_gate, w_up):
+    piece = chip_rows(w_gate, w_up)
+    rows, depth = piece.shape
+    tokens = normed.shape[0]
+    sems = pltpu.SemaphoreType.DMA
+    hidden = pl.pallas_call(
+        projection_kernel,
+        out_shape=jax.ShapeDtypeStruct((CHIPS, tokens, rows), jnp.bfloat16),
+        in_specs=[pl.BlockSpec(memory_space=pltpu.VMEM)] * 2,
+        out_specs=pl.BlockSpec(memory_space=pltpu.VMEM),
+        scratch_shapes=[
+            pltpu.VMEM((2, CHIPS, rows, depth), jnp.bfloat16),
+            sems((2, 3)),
+            sems((2, 6)),
+            sems((2, 6)),
+            sems((2, CHIPS)),
+            sems,
+        ],
+        compiler_params=pltpu.CompilerParams(
+            collective_id=0, has_side_effects=True, vmem_limit_bytes=48 * 2**20
+        ),
+        cost_estimate=pl.CostEstimate(
+            flops=4 * tokens * CHIPS * rows * depth,
+            bytes_accessed=2 * CHIPS * rows * depth * 2,
+            transcendentals=tokens * CHIPS * rows,
+        ),
+    )(normed, piece)
+    return hidden.transpose(1, 0, 2).reshape(tokens, CHIPS * rows)
 
 
 def per_device(x_in, gate_in, keys_b, queries_c, decay_log, level_mix, norm_gain, w_gate, w_up):
@@ -95,7 +296,8 @@
     own_prefix = jnp.zeros((head_count,), jnp.float32)
     device_levels = []
     for bit_index in range(seq_bits):
-        other_state, other_decay = swapped((summary, summary_decay), "seq", bit_index)
+        other_state, other_decay = swapped((summary.astype(jnp.bfloat16), summary_decay), "seq", bit_index)
+        other_state = other_state.astype(jnp.float32)
         is_upper = rank_here >> bit_index & 1 == 1
         device_levels.append(
             jnp.where(is_upper, jnp.exp(own_prefix)[:, None, None] * other_state, 0.0)
@@ -122,23 +324,9 @@
     normed = (
         gated * lax.rsqrt(jnp.mean(gated * gated, axis=-1, keepdims=True) + EPS) * norm_gain
     ).astype(jnp.bfloat16)
-    paired = jnp.stack([w_gate, w_up])
-    dp_count = lax.axis_size("dp")
-    seq_count = lax.axis_size("seq")
-    seq_weights = lax.all_gather(paired, "seq", axis=2, tiled=True)
-    projected = jnp.einsum(
-        "td,gdk->gtk",
-        normed,
-        lax.all_gather(seq_weights, "dp", axis=2, tiled=True),
-        preferred_element_type=jnp.float32,
-    )
-    returned = (jax.nn.silu(projected[0]) * projected[1]).astype(jnp.bfloat16)
-    hidden = (
-        returned.reshape(tok_dev, dp_count, seq_count, -1)
-        .transpose(0, 2, 1, 3)
-        .reshape(tok_dev, -1)
-    )
-    return hidden[None]
+    if (lax.axis_size("seq"), lax.axis_size("dp")) == (SEQ_COUNT, DP_COUNT):
+        return streamed_projection(normed, w_gate, w_up)[None]
+    return gathered_projection(normed, w_gate, w_up)[None]
 
 
 def solution(mesh):

time: 269 us -> 216 us (0.80)
  waiting for transfers between devices: 195 us -> 35.4 us
  Pallas kernels: 0 us -> 131 us
  matrix products: 32 us -> 15.4 us
  between operations: 13.6 us -> 0.26 us
    pallas_call x0 -> x1, Pallas kernels: none -> 131 us  [streamed_projection(): pl.pallas_call(projection_kernel, out_shape=jax.ShapeDtypeStruct((CHIPS,...]
    all_gather x2 -> x0, waiting for transfers between devices: 130 us -> none  [the longest x1 96.3 us: per_device(): seq_weights = lax.all_gather(paired, 'seq', axis=2, tiled=True)]
    ppermute x5, waiting for transfers between devices: 64.7 us -> 35.4 us  [swapped(): return lax.ppermute(value, axis, pairs)]
    dot_general x1 -> x0, matrix products: 12.2 us -> none  [per_device(): jnp.einsum('td,gdk->gtk', normed, lax.all_gather(seq_weights, 'dp', axis=...]
    add x2 -> x0, other arithmetic: 4.87 us -> none  [per_device(): summary = jnp.exp(upper_decay)[:, None, None] * lower_state + upper_state]
    select_n x0 -> x2, other arithmetic: none -> 3.46 us  [the longest x1 1.91 us: chip_rows(): other = lax.ppermute(jnp.where(first, up, gate), 'dp', pairs)]
    convert_element_type x1 -> x3, other arithmetic: 0.81 us -> 3.56 us  [the longest x1 2.05 us: per_device(): normed = (gated * lax.rsqrt(jnp.mean(gated * gated, axis=-1, keepdims=Tru...]
  transfers between devices with their start and end apart: 7 -> 6, of which waited for: 6 -> 3; matrix products, arithmetic and copies ran while one was open for 14% -> 12% of each run, Pallas kernels for 0% -> 0%
where the time goes in v1:
time: 216 us; the launch traced here: 215 us
  Pallas kernels  131 us (61%)
  waiting for transfers between devices  35.4 us (16%)
  matrix products  15.4 us (7%)
  local copies, waits for them, and re-layouts  13.8 us (6%)
  other arithmetic  11.1 us (5%)
  starting transfers between devices  7.78 us (4%)
    pallas_call x1, Pallas kernels, streamed_projection(): pl.pallas_call(projection_kernel, out_shape=jax.ShapeDtypeStruct((CHIPS,...  131 us
    ppermute x5, waiting for transfers between devices, swapped(): return lax.ppermute(value, axis, pairs)  35.4 us
    ppermute x5, starting transfers between devices, swapped(): return lax.ppermute(value, axis, pairs)  7.78 us
    dot_general x1, matrix products, block_inner(): chosen = jnp.einsum('lht,lts->hts', mix_low, level_picks, precision=HIGH)  6.46 us
  transfers between devices with their start and end apart: 6, of which 3 were waited for; matrix products, arithmetic and copies ran while one was open for 12% of the time, Pallas kernels for 0%

profile of v1, /device:TPU:0, one launch (start us, length us, event | category | flops | bytes accessed | tf_op | source)
XLA Modules:
  0.0 214.7 jit_solution(1513307576176373377)
XLA Ops:
  0.0 0.8 reshape.128
  0.8 0.6 reduce-window.6
  1.4 0.2 slice_reduce_fusion
  1.6 0.1 copy_bitcast_fusion
  1.7 0.2 slice_reduce_fusion.1
  1.9 3.0 %collective-permute-start.1 = (f32[32]{0:T(128)S(1)}, f32[32]{0:T(128)S(1)}, u32[]{:S(2)}, u32[]{:S(2)}) collective-permute-start(f32[32]{0:T(128)S(1)} %slice_reduce_fusion.1), channel_id=1, source_target_pairs={{0,4},{4,0},{8,12},{12,8},{16,20},{20,16},{24,28},{28,24},{1,5},{5... | collective-permute-start | bytes 392 | tf_op jit(solution)/shard_map/ppermute | solution.py:19
  4.9 1.9 broadcast_select_fusion
  6.8 0.0 collective-permute-start.5
  6.8 0.1 copy.26
  6.9 1.5 fusion.50
  8.5 0.7 iota_compare_fusion.4
  9.1 1.1 convert_reduce_fusion
  10.3 0.0 copy-done
  10.3 0.2 fusion.45
  10.5 0.0 copy-start.11
  10.5 1.5 copy.27
  12.0 2.5 %copy.33 = f32[1,9,32,256]{2,1,3,0:T(8,128)} copy(f32[1,9,32,256]{3,2,1,0:T(8,128)S(1)} %slice-done) | data formatting | bytes 589824
  14.5 0.0 collective-permute-done.1
  14.5 0.0 copy-done.11
  14.5 1.4 fusion.59
  15.9 0.0 copy-start.2
  15.9 0.1 collective-permute-start
  16.0 0.0 copy-done.6
  16.1 6.5 %fusion.1 = bf16[32,256,256]{2,0,1:T(8,128)(2,1)S(1)} fusion(f32[256,256]{1,0:T(8,128)S(1)} %fusion.45, f32[32,256]{1,0:T(8,128)S(1)} %copy_bitcast_fusion, f32[32,256]{0,1:T(8,128)S(1)} %copy.26, pred[256,256]{1,0:T(8,128)(4,1)S(1)} %copy-done.8, f32[1,9,32,256]{2,1,3,0:T(8,128)S(1)} %copy-done.6, s32[256,256]{1,0:T(8,128)S(1)} %add_select_fusion), kind=kOutput, calls=%fused_computation.2 | convolution fusion | flops 237568000 | bytes 5144576 | tf_op jit(solution)/shard_map/lht,lts->hts/dot_general | solution.py:37
  22.5 7.8 %collective-permute-done = bf16[32,128,64]{1,2,0:T(8,128)(2,1)S(1)} collective-permute-done((bf16[32,128,64]{1,2,0:T(8,128)(2,1)S(1)}, bf16[32,128,64]{1,2,0:T(8,128)(2,1)S(1)}, u32[]{:S(2)}, u32[]{:S(2)}) %collective-permute-start) | collective-permute-done | bytes 524320 | tf_op jit(solution)/shard_map/ppermute | solution.py:19
  30.3 1.1 fusion.29
  31.4 1.6 collective-permute-start.2
  33.0 3.8 %fusion.2 = f32[32,256,64]{1,2,0:T(8,128)} fusion(bf16[256,32,64]{0,2,1:T(8,128)(2,1)S(1)} %bitcast.110, bf16[32,256,256]{2,0,1:T(8,128)(2,1)S(1)} %fusion.1), kind=kOutput, calls=%fused_computation.5 | convolution fusion | flops 268435456 | bytes 7340032 | tf_op jit(solution)/shard_map/hts,shp->thp/dot_general | solution.py:42
  36.8 0.5 collective-permute-start.3
  37.3 0.0 copy-done.1
  37.3 1.6 copy.30
  38.9 6.3 %collective-permute-done.3 = f32[32]{0:T(128)S(1)} collective-permute-done((f32[32]{0:T(128)S(1)}, f32[32]{0:T(128)S(1)}, u32[]{:S(2)}, u32[]{:S(2)}) %collective-permute-start.3) | collective-permute-done | bytes 160 | tf_op jit(solution)/shard_map/ppermute | solution.py:19
  45.2 0.0 collective-permute-done.5
  45.3 1.6 maximum_select_fusion.piece
  46.8 0.0 collective-permute-done.2
  46.8 0.0 copy-done.3
  46.8 0.5 fusion.28
  47.3 2.6 %collective-permute-start.4 = (bf16[32,128,64]{1,2,0:T(8,128)(2,1)S(1)}, bf16[32,128,64]{1,2,0:T(8,128)(2,1)S(1)}, u32[]{:S(2)}, u32[]{:S(2)}) collective-permute-start(bf16[32,128,64]{1,2,0:T(8,128)(2,1)S(1)} %fusion.28), channel_id=1, source_target_pairs={{0,16},{4,20},{8,24},{12,28},{16,0},{20,4},{24,8},{28,12},{1,17},{... | collective-permute-start | bytes 1572872 | tf_op jit(solution)/shard_map/ppermute | solution.py:19
  50.0 0.4 fusion.32
  50.4 0.5 fusion.30
  50.9 21.2 %collective-permute-done.4 = bf16[32,128,64]{1,2,0:T(8,128)(2,1)S(1)} collective-permute-done((bf16[32,128,64]{1,2,0:T(8,128)(2,1)S(1)}, bf16[32,128,64]{1,2,0:T(8,128)(2,1)S(1)}, u32[]{:S(2)}, u32[]{:S(2)}) %collective-permute-start.4) | collective-permute-done | bytes 524320 | tf_op jit(solution)/shard_map/ppermute | solution.py:19
  72.1 0.0 copy-done.4
  72.2 2.6 %multiply_reduce_fusion = (f32[256]{0:T(256)S(1)}, f32[256,32,64]{0,2,1:T(8,128)}) fusion(f32[256,32,64]{0,2,1:T(8,128)S(1)} %bitcast.111, bf16[1,256,128]{2,1,0:T(8,128)(2,1)S(1)} %copy-done, bf16[32,128,64]{1,2,0:T(8,128)(2,1)S(1)} %collective-permute-done.4, f32[32]{0:T(128)S(1)} %get-tuple-element.11, pred[]{:T(512)S(6)} %eq.32, ...), kind=kOutput, calls=%fused_computation.26 | convolution fusion | flops 142081792 | bytes 11175041 | tf_op jit(solution)/shard_map/tn,hnp->thp/dot_general | solution.py:54
  74.7 2.1 copy.29
  76.9 2.0 fusion.19.normed
  78.9 130.9 %shard_map.91 = bf16[16,256,176]{2,1,0:T(8,128)(2,1)S(1)} custom-call(bf16[256,2048]{1,0:T(8,128)(2,1)S(1)} %fusion.19.normed, bf16[176,2048]{1,0:T(8,128)(2,1)S(1)} %maximum_select_fusion.piece), custom_call_target="tpu_custom_call" | custom-call | flops 5905580032 | bytes 23068672 | tf_op jit(solution)/shard_map/pallas_call | solution.py:238
  209.9 2.3 %copy.31 = bf16[256,16,176]{0,2,1:T(8,128)(2,1)} copy(bf16[256,16,176]{2,0,1:T(8,128)(2,1)S(1)} %bitcast.107) | data formatting | bytes 2883584 | tf_op jit(solution)/shard_map/transpose | solution.py:260
  212.1 2.5 %copy.32 = bf16[1,256,2816]{2,1,0:T(8,128)(2,1)} copy(bf16[1,256,2816]{1,2,0:T(8,128)(2,1)} %bitcast.108) | data formatting | bytes 2883584 | tf_op jit(solution)/shard_map/broadcast_in_dim;reshape | solution.py:328
  (30 shorter events, 0.2 us)
Async XLA Ops:
  0.0 10.3 %copy-start = (bf16[1,256,128]{2,1,0:T(8,128)(2,1)S(1)}, bf16[1,256,128]{2,1,0:T(8,128)(2,1)}, u32[]{:S(2)}) copy-start(bf16[1,256,128]{2,1,0:T(8,128)(2,1)} %param.12) | copy-start | bytes 196612
  0.0 9.1 %copy-start.7 = (bf16[1,256,128]{2,1,0:T(8,128)(2,1)S(1)}, bf16[1,256,128]{2,1,0:T(8,128)(2,1)}, u32[]{:S(2)}) copy-start(bf16[1,256,128]{2,1,0:T(8,128)(2,1)} %param.11) | copy-start | bytes 196612
  1.9 12.6 %collective-permute-start.1 = (f32[32]{0:T(128)S(1)}, f32[32]{0:T(128)S(1)}, u32[]{:S(2)}, u32[]{:S(2)}) collective-permute-start(f32[32]{0:T(128)S(1)} %slice_reduce_fusion.1), channel_id=1, source_target_pairs={{0,4},{4,0},{8,12},{12,8},{16,20},{20,16},{24,28},{28,24},{1,5},{5... | collective-permute-start | bytes 392 | tf_op jit(solution)/shard_map/ppermute | solution.py:19
  6.8 38.4 %collective-permute-start.5 = (bf16[88,2048]{1,0:T(8,128)(2,1)}, bf16[88,2048]{1,0:T(8,128)(2,1)}, u32[]{:S(2)}, u32[]{:S(2)}) collective-permute-start(bf16[88,2048]{1,0:T(8,128)(2,1)} %broadcast_select_fusion), channel_id=1, source_target_pairs={{0,1},{1,0},{2,3},{3,2},{4,5},{5,4},{6,7},{7,6},{8,9},{9,8},{10,11... | collective-permute-start | bytes 1081352 | tf_op jit(solution)/shard_map/ppermute | solution.py:229
  8.4 3.5 %slice-start = ((f32[1,12,32,256]{3,2,1,0:T(8,128)}), f32[1,9,32,256]{3,2,1,0:T(8,128)S(1)}, s32[]{:S(2)}) async-start(f32[1,12,32,256]{3,2,1,0:T(8,128)} %param.14), calls=%async_computation | async-start | bytes 589824 | tf_op jit(solution)/shard_map/slice | solution.py:283
  10.5 4.0 %copy-start.11 = (f32[256,32]{0,1:T(8,128)S(1)}, f32[256,32]{0,1:T(8,128)}, u32[]{:S(2)}) copy-start(f32[256,32]{0,1:T(8,128)} %get-tuple-element.8) | copy-start | bytes 98308
  14.5 1.6 copy-start.6
  14.5 1.6 copy-start.8
  15.9 14.4 %copy-start.2 = (f32[32,128,64]{1,2,0:T(8,128)}, f32[32,128,64]{1,2,0:T(8,128)S(1)}, u32[]{:S(2)}) copy-start(f32[32,128,64]{1,2,0:T(8,128)S(1)} %get-tuple-element.16) | copy-start | bytes 3145732
  15.9 14.4 %collective-permute-start = (bf16[32,128,64]{1,2,0:T(8,128)(2,1)S(1)}, bf16[32,128,64]{1,2,0:T(8,128)(2,1)S(1)}, u32[]{:S(2)}, u32[]{:S(2)}) collective-permute-start(bf16[32,128,64]{1,2,0:T(8,128)(2,1)S(1)} %get-tuple-element.15), channel_id=1, source_target_pairs={{0,4},{4,0},{8,12},{12,8},{16,20},{20,16},{24,28},{28,24},{1,5},{5... | collective-permute-start | bytes 1572872 | tf_op jit(solution)/shard_map/ppermute | solution.py:19
  31.4 5.9 %copy-start.1 = (bf16[1,256,2048]{2,1,0:T(8,128)(2,1)S(1)}, bf16[1,256,2048]{2,1,0:T(8,128)(2,1)}, u32[]{:S(2)}) copy-start(bf16[1,256,2048]{2,1,0:T(8,128)(2,1)} %param.10) | copy-start | bytes 3145732
  31.4 15.4 %collective-permute-start.2 = (bf16[32,128,64]{1,2,0:T(8,128)(2,1)}, bf16[32,128,64]{1,2,0:T(8,128)(2,1)S(1)}, u32[]{:S(2)}, u32[]{:S(2)}) collective-permute-start(bf16[32,128,64]{1,2,0:T(8,128)(2,1)} %fusion.29), channel_id=1, source_target_pairs={{0,8},{4,12},{8,0},{12,4},{16,24},{20,28},{24,16},{28,20},{1,9},{5... | collective-permute-start | bytes 1572872 | tf_op jit(solution)/shard_map/ppermute | solution.py:19
  36.8 10.0 %copy-start.3 = (f32[32,128,64]{1,2,0:T(8,128)S(1)}, f32[32,128,64]{1,2,0:T(8,128)}, u32[]{:S(2)}) copy-start(f32[32,128,64]{1,2,0:T(8,128)} %copy-done.2) | copy-start | bytes 3145732
  36.8 8.4 %collective-permute-start.3 = (f32[32]{0:T(128)S(1)}, f32[32]{0:T(128)S(1)}, u32[]{:S(2)}, u32[]{:S(2)}) collective-permute-start(f32[32]{0:T(128)S(1)} %get-tuple-element.9), channel_id=1, source_target_pairs={{0,8},{4,12},{8,0},{12,4},{16,24},{20,28},{24,16},{28,20},{1,9},{5... | collective-permute-start | bytes 392 | tf_op jit(solution)/shard_map/ppermute | solution.py:19
  47.3 24.8 %copy-start.4 = (f32[32,256,64]{1,2,0:T(8,128)S(1)}, f32[32,256,64]{1,2,0:T(8,128)}, u32[]{:S(2)}) copy-start(f32[32,256,64]{1,2,0:T(8,128)} %fusion.2) | copy-start | bytes 6291460
  47.3 24.8 %copy-start.5 = (f32[1,256,2048]{1,2,0:T(8,128)S(1)}, f32[1,256,2048]{1,2,0:T(8,128)}, u32[]{:S(2)}) copy-start(f32[1,256,2048]{1,2,0:T(8,128)} %copy.30) | copy-start | bytes 6291460
  47.3 24.8 %copy-start.9 = (f32[256,32]{0,1:T(8,128)S(1)}, f32[256,32]{0,1:T(8,128)}, u32[]{:S(2)}) copy-start(f32[256,32]{0,1:T(8,128)} %get-tuple-element.6) | copy-start | bytes 98308
  47.3 24.8 %copy-start.10 = (f32[256,32]{0,1:T(8,128)S(1)}, f32[256,32]{0,1:T(8,128)}, u32[]{:S(2)}) copy-start(f32[256,32]{0,1:T(8,128)} %get-tuple-element.7) | copy-start | bytes 98308
  47.3 24.8 %collective-permute-start.4 = (bf16[32,128,64]{1,2,0:T(8,128)(2,1)S(1)}, bf16[32,128,64]{1,2,0:T(8,128)(2,1)S(1)}, u32[]{:S(2)}, u32[]{:S(2)}) collective-permute-start(bf16[32,128,64]{1,2,0:T(8,128)(2,1)S(1)} %fusion.28), channel_id=1, source_target_pairs={{0,16},{4,20},{8,24},{12,28},{16,0},{20,4},{24,8},{28,12},{1,17},{... | collective-permute-start | bytes 1572872 | tf_op jit(solution)/shard_map/ppermute | solution.py:19
  74.7 2.1 copy-start.12

commit v2 on v1

--- a/solution.py
+++ b/solution.py
@@ -100,6 +100,7 @@
         self.piece, self.held, self.own_sem = piece, held, own_sem
         self.sems = {"z": z_sems, "x": x_sems, "y": y_sems, "core": core_sems}
         seq, dp = lax.axis_index("seq"), lax.axis_index("dp")
+        self.seq, self.dp = seq, dp
         self.z, self.x, self.y, self.core = seq // 2, lax.rem(seq, 2), dp // 2, lax.rem(dp, 2)
         self.targets = {
             "z": (line_member(self.z, -1) * 2 + self.x, dp),
@@ -108,6 +109,9 @@
             "core": (seq, self.y * 2 + 1 - self.core),
         }
         self.before = (line_member(self.z, 1) * 2 + self.x, dp)
+        rows = piece.shape[0]
+        cut = (rows // 2 + 15) // 16 * 16
+        self.cuts = ((0, cut), (cut, rows - cut))
         self.sent = []
 
     def greet(self):
@@ -122,10 +126,11 @@
         y = 1 - self.y if flip_y else self.y
         return line_member(self.z, step) * 4 + x * 2 + y
 
-    def copy(self, way, slot, chip, own=False):
-        place = self.held.at[self.core, chip]
+    def copy(self, way, slot, chip, part, own=False):
+        first, count = self.cuts[part]
+        place = self.held.at[self.core, chip, pl.ds(first, count)]
         return pltpu.make_async_remote_copy(
-            src_ref=self.piece if own else place,
+            src_ref=self.piece.at[pl.ds(first, count)] if own else place,
             dst_ref=place,
             send_sem=self.sems[way].at[0, slot],
             recv_sem=self.sems[way].at[1, slot],
@@ -133,8 +138,8 @@
             device_id_type=MESH,
         )
 
-    def send(self, way, slot, chip, own=False):
-        copy = self.copy(way, slot, chip, own)
+    def send(self, way, slot, chip, part, own=False):
+        copy = self.copy(way, slot, chip, part, own)
         copy.start()
         self.sent.append(copy)
 
@@ -143,48 +148,56 @@
         self.own = pltpu.make_async_copy(self.piece, self.held.at[self.core, chip], self.own_sem)
         self.own.start()
         for way in ("z", "x", "y", "core"):
-            self.send(way, 0, chip, own=True)
-
-    def line(self, step):
+            for part in range(2):
+                self.send(way, part, chip, part, own=True)
+
+    def line(self, step, part):
         chip = self.chip(step, 0, 0)
-        self.copy("z", step - 1, chip).wait_recv()
+        self.copy("z", (step - 1) * 2 + part, chip, part).wait_recv()
         if step < LINE - 1:
-            self.send("z", step, chip)
+            self.send("z", step * 2 + part, chip, part)
         for way in ("x", "y"):
-            self.send(way, step, chip)
-        self.send("core", step * 4, chip)
-
-    def across_x(self, step):
+            self.send(way, step * 2 + part, chip, part)
+        self.send("core", step * 8 + part, chip, part)
+
+    def across_x(self, step, part):
         chip = self.chip(step, 1, 0)
-        self.copy("x", step, chip).wait_recv()
-        if step < 2:
-            self.send("y", LINE + step, chip)
-        self.send("core", step * 4 + 1, chip)
-
-    def across_y(self, step):
+        self.copy("x", step * 2 + part, chip, part).wait_recv()
+        if part == 0:
+            self.send("y", 2 * LINE + step, chip, part)
+        self.send("core", step * 8 + 2 + part, chip, part)
+
+    def across_y(self, step, part):
         chip = self.chip(step, 0, 1)
-        self.copy("y", step, chip).wait_recv()
-        if step >= 2:
-            self.send("x", LINE + step - 2, chip)
-        self.send("core", step * 4 + 2, chip)
+        self.copy("y", step * 2 + part, chip, part).wait_recv()
+        if part == 1:
+            self.send("x", 2 * LINE + step, chip, part)
+        self.send("core", step * 8 + 4 + part, chip, part)
+
+    def across(self, step, part):
+        self.across_x(step, part)
+        self.across_y(step, part)
 
     def corner(self, step):
         chip = self.chip(step, 1, 1)
-        way = "y" if step < 2 else "x"
-        self.copy(way, LINE + step % 2, chip).wait_recv()
-        self.send("core", step * 4 + 3, chip)
+        for part, way in enumerate(("y", "x")):
+            self.copy(way, 2 * LINE + step, chip, part).wait_recv()
+            self.send("core", step * 8 + 6 + part, chip, part)
 
     def ready(self, step, kind):
         chip = self.chip(step, kind % 2, kind // 2)
-        place = self.held.at[1 - self.core, chip]
-        pltpu.make_async_remote_copy(
-            src_ref=place,
-            dst_ref=place,
-            send_sem=self.sems["core"].at[0, step * 4 + kind],
-            recv_sem=self.sems["core"].at[1, step * 4 + kind],
-            device_id=self.targets["core"],
-            device_id_type=MESH,
-        ).wait_recv()
+        for part in range(2):
+            first, count = self.cuts[part]
+            place = self.held.at[1 - self.core, chip, pl.ds(first, count)]
+            slot = step * 8 + kind * 2 + part
+            pltpu.make_async_remote_copy(
+                src_ref=place,
+                dst_ref=place,
+                send_sem=self.sems["core"].at[0, slot],
+                recv_sem=self.sems["core"].at[1, slot],
+                device_id=self.targets["core"],
+                device_id_type=MESH,
+            ).wait_recv()
         return chip
 
     def finish(self):
@@ -192,34 +205,241 @@
             copy.wait_send()
 
 
-def project(normed, held, hidden, chip):
-    contract = (((1,), (1,)), ((), ()))
-    gate = lax.dot_general(normed[...], held[0, chip], contract, preferred_element_type=jnp.float32)
-    up = lax.dot_general(normed[...], held[1, chip], contract, preferred_element_type=jnp.float32)
-    hidden[chip] = (gate / (1.0 + jnp.exp(-gate)) * up).astype(hidden.dtype)
-
-
-def projection_kernel(normed, piece, hidden, held, z_sems, x_sems, y_sems, core_sems, own_sem):
+NT = (((1,), (1,)), ((), ()))
+HALF = SPAN // 2
+GROUP = 4
+
+
+def rows_of(index, count):
+    return pl.ds(pl.multiple_of(index * count, count), count)
+
+
+def layer_kernel(
+    x_in, gate_in, keys, queries, decay, mix, gain, piece, hidden,
+    held, x_cols, gate_cols, normed, mixed, run_col, run_row, tail, level_scale,
+    level_of, scores, state, state_out, state_in, decay_out, decay_in,
+    z_sems, x_sems, y_sems, core_sems, own_sem, state_sems, decay_sems,
+):
     gather = Gather(piece, held, z_sems, x_sems, y_sems, core_sems, own_sem)
     gather.greet()
     gather.start()
+    heads = decay.shape[0]
+    head_dim = x_cols.shape[0] // heads
+    seq, dp = gather.seq, gather.dp
+    f32, bf16 = jnp.float32, jnp.bfloat16
+
+    def exchange(bit):
+        target = (seq + (1 - 2 * (seq // 2**bit % 2)) * 2**bit, dp)
+        pairs = [(state_out, state_in, state_sems), (decay_out, decay_in, decay_sems)]
+        return [
+            pltpu.make_async_remote_copy(
+                src_ref=source.at[bit],
+                dst_ref=place.at[bit],
+                send_sem=sems.at[0, bit],
+                recv_sem=sems.at[1, bit],
+                device_id=target,
+                device_id_type=MESH,
+            )
+            for source, place, sems in pairs[: 1 if bit == 2 else 2]
+        ]
+
+    before = lax.broadcasted_iota(jnp.int32, (SPAN, SPAN), 0)
+    after = lax.broadcasted_iota(jnp.int32, (SPAN, SPAN), 1)
+    up_to = (before <= after).astype(f32)
+    run = jnp.dot(decay[...], up_to, precision=HIGH, preferred_element_type=f32)
+    run_row[...] = run
+    tail[...] = jnp.exp(jnp.minimum(run[:, SPAN - 1 :] - run, 0.0))
+    total = jnp.broadcast_to(run[:, SPAN - 1 :], (heads, 128))
+    decay_out[0] = total
+
+    def turn(index, _):
+        lanes = rows_of(index, 128)
+        x_cols[lanes, :] = x_in[:, lanes].astype(f32).T.astype(bf16)
+        return 0
+
+    lax.fori_loop(0, x_cols.shape[0] // 128, turn, 0)
+
+    def block_states(index, _):
+        parts = []
+        for place in range(GROUP):
+            head = index * GROUP + place
+            values = x_cols[rows_of(head, head_dim), :].astype(f32) * tail[pl.ds(head, 1), :]
+            parts.append(values.astype(bf16))
+        rows = rows_of(index, GROUP * head_dim)
+        result = jnp.dot(jnp.concatenate(parts), keys[...], preferred_element_type=f32)
+        state[rows, :] = result
+        state_out[0, rows, :] = result.astype(bf16)
+        return 0
+
+    lax.fori_loop(0, heads // GROUP, block_states, 0)
+    rounds = [exchange(0)]
+    for copy in rounds[0]:
+        copy.start()
+
+    gather.line(1, 0)
+    gather.across(0, 0)
+
+    columns = lax.dot_general(
+        (before >= after).astype(f32), decay[...], NT, precision=HIGH, preferred_element_type=f32
+    )
+    for head in range(heads):
+        run_col[head] = jnp.broadcast_to(columns[:, head : head + 1], (SPAN, 128))
+    scores[...] = lax.dot_general(keys[...], queries[...], NT, preferred_element_type=f32)
+    source = lax.broadcasted_iota(jnp.int32, (HALF, HALF), 0)
+    target = lax.broadcasted_iota(jnp.int32, (HALF, HALF), 1)
+    differ = source ^ target
+    level = jnp.zeros((HALF, HALF), jnp.int32)
+    for bit in range(SPAN_BITS - 1):
+        level = level + (differ >= 2**bit).astype(jnp.int32)
+    level_of[...] = jnp.where(source <= target, level, -1)
+
+    gather.line(1, 1)
+    gather.across(0, 1)
+
+    def local(head, _):
+        run_t = run_row[pl.ds(head, 1), :]
+        mixes = [mix[rank, pl.ds(head, 1), :] for rank in range(SPAN_BITS + 1)]
+        values = x_cols[rows_of(head, head_dim), :]
+        weights = []
+        for first in (0, HALF):
+            span = slice(first, first + HALF)
+            gap = run_t[:, span] - run_col[head, span, :]
+            levels = level_of[...]
+            chosen = jnp.zeros((HALF, HALF), f32)
+            for rank in range(SPAN_BITS):
+                chosen = jnp.where(levels == rank, mixes[rank][:, span], chosen)
+            weights.append(chosen * jnp.exp(jnp.minimum(gap, 0.0)) * scores[span, span])
+        gap = run_t[:, HALF:] - run_col[head, :HALF, :]
+        cross = mixes[SPAN_BITS][:, HALF:] * jnp.exp(jnp.minimum(gap, 0.0))
+        cross = (cross * scores[:HALF, HALF:]).astype(bf16)
+        rows = rows_of(head, head_dim)
+        mixed[rows, :HALF] = jnp.dot(
+            values[:, :HALF], weights[0].astype(bf16), preferred_element_type=f32
+        )
+        mixed[rows, HALF:] = jnp.dot(
+            values, jnp.concatenate([cross, weights[1].astype(bf16)]), preferred_element_type=f32
+        )
+        return 0
+
+    def locals_of(quarter):
+        lax.fori_loop(quarter * heads // 4, (quarter + 1) * heads // 4, local, 0)
+
+    prefix = jnp.zeros((heads, 128), f32)
+
+    def scale_level(bit, prefix):
+        upper = (seq // 2**bit % 2).astype(f32)
+        growth = jnp.exp(run_row[...] + jnp.concatenate([prefix] * 2, axis=1))
+        level_scale[bit] = upper * mix[SPAN_BITS + 1 + bit] * growth
+
+    def merge(bit, total, prefix):
+        for copy in rounds[bit]:
+            copy.wait_recv()
+        other = decay_in[bit]
+        upper = (seq // 2**bit % 2).astype(f32)
+        scale_level(bit, prefix)
+        tail[:, :128] = jnp.exp((1.0 - upper) * other)
+        tail[:, 128:] = jnp.exp(upper * total)
+
+        def add(head, _):
+            rows = rows_of(head, head_dim)
+            factors = tail[pl.ds(head, 1), :]
+            mine = factors[:, :128] * state[rows, :]
+            both = mine + factors[:, 128:] * state_in[bit, rows, :].astype(f32)
+            state[rows, :] = both
+            state_out[bit + 1, rows, :] = both.astype(bf16)
+            return 0
+
+        lax.fori_loop(0, heads, add, 0)
+        total = total + other
+        if bit == 0:
+            decay_out[1] = total
+        rounds.append(exchange(bit + 1))
+        for copy in rounds[bit + 1]:
+            copy.start()
+        return total, prefix + upper * other
+
+    def distant(bit):
+        def add(index, _):
+            rows = rows_of(index, GROUP * head_dim)
+            product = lax.dot_general(
+                state_in[bit, rows, :], queries[...], NT, preferred_element_type=f32
+            )
+            for place in range(GROUP):
+                head = index * GROUP + place
+                part = product[place * head_dim : (place + 1) * head_dim]
+                mixed[rows_of(head, head_dim), :] += level_scale[bit, pl.ds(head, 1), :] * part
+            return 0
+
+        lax.fori_loop(0, heads // GROUP, add, 0)
+
+    locals_of(0)
+    gather.line(2, 0)
+    total, prefix = merge(0, total, prefix)
+    gather.across(1, 0)
+    locals_of(1)
+    gather.line(2, 1)
+    gather.across(1, 1)
+    locals_of(2)
+    gather.line(3, 0)
+    gather.corner(0)
+    total, prefix = merge(1, total, prefix)
+    scale_level(2, prefix)
+    gather.line(3, 1)
+    gather.across(2, 0)
+    locals_of(3)
+    gather.corner(1)
+    gather.across(2, 1)
+    distant(0)
+    distant(1)
+
+    def turn_gate(index, _):
+        lanes = rows_of(index, 128)
+        gate_cols[lanes, :] = gate_in[:, lanes].astype(f32).T.astype(bf16)
+        return 0
+
+    lax.fori_loop(0, gate_cols.shape[0] // 128, turn_gate, 0)
+    gather.across(3, 0)
+    gather.across(3, 1)
+    rounds[2][0].wait_recv()
+    distant(2)
+
+    def gated(index, squares):
+        rows = rows_of(index, head_dim)
+        gate = gate_cols[rows, :].astype(f32)
+        value = mixed[rows, :] * (gate / (1.0 + jnp.exp(-gate)))
+        mixed[rows, :] = value
+        return squares + jnp.sum(value * value, axis=0, keepdims=True)
+
+    squares = lax.fori_loop(0, heads, gated, jnp.zeros((1, SPAN), f32))
+    scale = lax.rsqrt(squares / mixed.shape[0] + EPS)
+
+    def norm(index, _):
+        rows = rows_of(index, head_dim)
+        normed[rows, :] = (mixed[rows, :] * scale * gain[rows, :]).astype(bf16)
+        return 0
+
+    lax.fori_loop(0, heads, norm, 0)
+
+    def project(chip):
+        gate = jnp.dot(held[0, chip], normed[...], preferred_element_type=f32)
+        up = jnp.dot(held[1, chip], normed[...], preferred_element_type=f32)
+        hidden[chip] = (gate / (1.0 + jnp.exp(-gate)) * up).astype(bf16)
+
     gather.own.wait()
-    project(normed, held, hidden, gather.ready(0, 0))
-    for step in range(LINE):
-        gather.across_x(step)
-        gather.across_y(step)
-        if step + 1 < LINE:
-            gather.line(step + 1)
-        project(normed, held, hidden, gather.ready(step, 1))
-        project(normed, held, hidden, gather.ready(step, 2))
-        if step >= 1:
-            gather.corner(step - 1)
-            project(normed, held, hidden, gather.ready(step - 1, 3))
-        if step + 1 < LINE:
-            project(normed, held, hidden, gather.ready(step + 1, 0))
-    gather.corner(LINE - 1)
-    project(normed, held, hidden, gather.ready(LINE - 1, 3))
+    for step in range(LINE - 1):
+        for kind in range(4):
+            if (step, kind) != (2, 3):
+                project(gather.ready(step, kind))
+    gather.corner(2)
+    for kind in range(3):
+        project(gather.ready(3, kind))
+    project(gather.ready(2, 3))
+    gather.corner(3)
+    project(gather.ready(3, 3))
     gather.finish()
+    for copies in rounds:
+        for copy in copies:
+            copy.wait_send()
 
 
 def chip_rows(w_gate, w_up):
@@ -230,37 +450,62 @@
     return jnp.where(first, jnp.concatenate([gate, other]), jnp.concatenate([other, up]))
 
 
-def streamed_projection(normed, w_gate, w_up):
+def streamed_layer(x, gate, keys, queries, decay, mix, norm_gain, w_gate, w_up):
     piece = chip_rows(w_gate, w_up)
     rows, depth = piece.shape
-    tokens = normed.shape[0]
+    tokens = x.shape[0]
+    heads = decay.shape[0]
+    states = keys.shape[1]
     sems = pltpu.SemaphoreType.DMA
+    f32, bf16 = jnp.float32, jnp.bfloat16
     hidden = pl.pallas_call(
-        projection_kernel,
-        out_shape=jax.ShapeDtypeStruct((CHIPS, tokens, rows), jnp.bfloat16),
-        in_specs=[pl.BlockSpec(memory_space=pltpu.VMEM)] * 2,
+        layer_kernel,
+        out_shape=jax.ShapeDtypeStruct((CHIPS, rows, tokens), bf16),
+        in_specs=[pl.BlockSpec(memory_space=pltpu.VMEM)] * 8,
         out_specs=pl.BlockSpec(memory_space=pltpu.VMEM),
         scratch_shapes=[
-            pltpu.VMEM((2, CHIPS, rows, depth), jnp.bfloat16),
+            pltpu.VMEM((2, CHIPS, rows, depth), bf16),
+            pltpu.VMEM((depth, tokens), bf16),
+            pltpu.VMEM((depth, tokens), bf16),
+            pltpu.VMEM((depth, tokens), bf16),
+            pltpu.VMEM((depth, tokens), f32),
+            pltpu.VMEM((heads, tokens, 128), f32),
+            pltpu.VMEM((heads, tokens), f32),
+            pltpu.VMEM((heads, tokens), f32),
+            pltpu.VMEM((3, heads, tokens), f32),
+            pltpu.VMEM((HALF, HALF), jnp.int32),
+            pltpu.VMEM((SPAN, SPAN), f32),
+            pltpu.VMEM((depth, states), f32),
+            pltpu.VMEM((3, depth, states), bf16),
+            pltpu.VMEM((3, depth, states), bf16),
+            pltpu.VMEM((2, heads, 128), f32),
+            pltpu.VMEM((2, heads, 128), f32),
+            sems((2, 6)),
+            sems((2, 12)),
+            sems((2, 12)),
+            sems((2, 2 * CHIPS)),
+            sems,
             sems((2, 3)),
-            sems((2, 6)),
-            sems((2, 6)),
-            sems((2, CHIPS)),
-            sems,
+            sems((2, 2)),
         ],
         compiler_params=pltpu.CompilerParams(
-            collective_id=0, has_side_effects=True, vmem_limit_bytes=48 * 2**20
+            collective_id=0, has_side_effects=True, vmem_limit_bytes=56 * 2**20
         ),
         cost_estimate=pl.CostEstimate(
             flops=4 * tokens * CHIPS * rows * depth,
             bytes_accessed=2 * CHIPS * rows * depth * 2,
             transcendentals=tokens * CHIPS * rows,
         ),
-    )(normed, piece)
-    return hidden.transpose(1, 0, 2).reshape(tokens, CHIPS * rows)
+    )(x, gate, keys, queries, decay, mix, norm_gain[:, None], piece)
+    return hidden.reshape(CHIPS * rows, tokens).T
 
 
 def per_device(x_in, gate_in, keys_b, queries_c, decay_log, level_mix, norm_gain, w_gate, w_up):
+    mesh_sizes = (lax.axis_size("seq"), lax.axis_size("dp"))
+    if mesh_sizes == (SEQ_COUNT, DP_COUNT) and x_in.shape[1] == SPAN:
+        local = (x_in, gate_in, keys_b, queries_c, decay_log, level_mix)
+        layer = streamed_layer(*(array[0] for array in local), norm_gain, w_gate, w_up)
+        return layer[None]
     tok_dev = x_in.shape[1]
     embedding_width = x_in.shape[2]
     head_count = decay_log.shape[1]
@@ -324,8 +569,6 @@
     normed = (
         gated * lax.rsqrt(jnp.mean(gated * gated, axis=-1, keepdims=True) + EPS) * norm_gain
     ).astype(jnp.bfloat16)
-    if (lax.axis_size("seq"), lax.axis_size("dp")) == (SEQ_COUNT, DP_COUNT):
-        return streamed_projection(normed, w_gate, w_up)[None]
     return gathered_projection(normed, w_gate, w_up)[None]
 
 

time: 216 us -> 123 us (0.57)
  waiting for transfers between devices: 35.4 us -> 0.01 us
  matrix products: 15.4 us -> 0 us
  Pallas kernels: 131 us -> 116 us
  local copies, waits for them, and re-layouts: 13.8 us -> 4.58 us
  other arithmetic: 11.1 us -> 2.26 us
  starting transfers between devices: 7.78 us -> 0.52 us
    ppermute x5 -> x0, waiting for transfers between devices: 35.4 us -> none  [swapped(): return lax.ppermute(value, axis, pairs)]
    dot_general x7 -> x0, matrix products: 15.4 us -> none  [the longest x1 6.46 us: block_inner(): chosen = jnp.einsum('lht,lts->hts', mix_low, level_picks, precision=HIGH)]
    pallas_call x1, Pallas kernels: 131 us -> 116 us  [streamed_layer(): pl.pallas_call(layer_kernel, out_shape=jax.ShapeDtypeStruct((CHIPS, rows,...]
    ppermute x5 -> x0, starting transfers between devices: 7.78 us -> none  [swapped(): return lax.ppermute(value, axis, pairs)]
    unnamed x28 -> x4, local copies, waits for them, and re-layouts: 4.03 us -> 0.01 us
    convert_element_type x4 -> x0, other arithmetic: 3.57 us -> none  [the longest x1 2.05 us: per_device(): normed = (gated * lax.rsqrt(jnp.mean(gated * gated, axis=-1, keepdims=Tru...]
    another operation x3 -> x0, local copies, waits for them, and re-layouts: 2.63 us -> none  [the longest x1 2.53 us: per_device(): return streamed_projection(normed, w_gate, w_up)[None]]
    transpose x1 -> x0, local copies, waits for them, and re-layouts: 2.27 us -> none  [streamed_projection(): return hidden.transpose(1, 0, 2).reshape(tokens, CHIPS * rows)]
  transfers between devices with their start and end apart: 6 -> 1, of which waited for: 3 -> 0; matrix products, arithmetic and copies ran while one was open for 12% -> 2% of each run, Pallas kernels for 0% -> 0%
where the time goes in v2:
time: 123 us
  Pallas kernels  116 us (94%)
  local copies, waits for them, and re-layouts  4.58 us (4%)
  other arithmetic  2.26 us (2%)
    pallas_call x1, Pallas kernels, streamed_layer(): pl.pallas_call(layer_kernel, out_shape=jax.ShapeDtypeStruct((CHIPS, rows,...  116 us
    reshape x1, local copies, waits for them, and re-layouts, streamed_layer(): return hidden.reshape(CHIPS * rows, tokens).T  2.53 us
  transfers between devices with their start and end apart: 1, of which 0 were waited for; matrix products, arithmetic and copies ran while one was open for 2% of the time, Pallas kernels for 0%

profile of v2, /device:TPU:0, one launch (start us, length us, event | category | flops | bytes accessed | tf_op | source)
XLA Modules:
  0.0 123.2 jit_solution(15755134223139113933)
XLA Ops:
  0.0 0.0 copy-start
  0.0 0.0 copy-start.1
  0.0 1.2 broadcast_select_fusion
  1.2 0.5 collective-permute-start
  1.7 2.0 %copy.11.gain = f32[2048,1]{1,0:T(8,128)} copy(f32[2048,1]{0,1:T(1,128)} %bitcast.18) | data formatting | bytes 16384 | tf_op jit(solution)/shard_map/broadcast_in_dim | solution.py:499
  3.8 0.0 collective-permute-done
  3.8 0.0 copy-done
  3.8 0.0 copy-done.1
  3.8 1.1 maximum_select_fusion.piece
  4.8 115.8 %shard_map.91 = bf16[16,176,256]{2,1,0:T(8,128)(2,1)} custom-call(bf16[256,2048]{1,0:T(8,128)(2,1)} %bitcast.19, bf16[256,2048]{1,0:T(8,128)(2,1)} %bitcast.20, bf16[256,128]{1,0:T(8,128)(2,1)} %bitcast.22, bf16[256,128]{1,0:T(8,128)(2,1)} %bitcast.23, f32[32,256]{1,0:T(8,128)} %bitcast.24, f32[12,32,256]{2,1,0:T(8,128)} %bitcast.21, f32[2048,1]{1,0:T(8,128)} %copy.11.gain, ...), custom_call_target="tpu_custom_call" | custom-call | flops 5905580032 | bytes 23068672 | tf_op jit(solution)/shard_map/pallas_call | solution.py:461
  120.7 2.5 %copy.12 = bf16[2816,256]{0,1:T(8,128)(2,1)} copy(bf16[2816,256]{1,0:T(8,128)(2,1)} %bitcast.15) | data formatting | bytes 2883584 | tf_op jit(solution)/shard_map/reshape | solution.py:500
Async XLA Ops:
  0.0 3.8 %copy-start = (bf16[2048,88]{0,1:T(8,128)(2,1)S(1)}, bf16[2048,88]{0,1:T(8,128)(2,1)}, u32[]{:S(2)}) copy-start(bf16[2048,88]{0,1:T(8,128)(2,1)} %param.17) | copy-start | bytes 1081348
  0.0 3.8 %copy-start.1 = (bf16[2048,88]{0,1:T(8,128)(2,1)S(1)}, bf16[2048,88]{0,1:T(8,128)(2,1)}, u32[]{:S(2)}) copy-start(bf16[2048,88]{0,1:T(8,128)(2,1)} %param.16) | copy-start | bytes 1081348
  1.2 2.6 %collective-permute-start = (bf16[88,2048]{1,0:T(8,128)(2,1)S(1)}, bf16[88,2048]{1,0:T(8,128)(2,1)S(1)}, u32[]{:S(2)}, u32[]{:S(2)}) collective-permute-start(bf16[88,2048]{1,0:T(8,128)(2,1)S(1)} %broadcast_select_fusion), channel_id=1, source_target_pairs={{0,1},{1,0},{2,3},{3,2},{4,5},{5,4},{6,7},{7,6},{8,9},{9,8},{10,11... | collective-permute-start | bytes 1081352 | tf_op jit(solution)/shard_map/ppermute | solution.py:449

commit v3 on v2

--- a/solution.py
+++ b/solution.py
@@ -87,6 +87,7 @@
 DP_COUNT = 4
 LINE = 4
 CHIPS = 16
+PARTS = 3
 
 
 def line_member(z, steps):
@@ -110,8 +111,8 @@
         }
         self.before = (line_member(self.z, 1) * 2 + self.x, dp)
         rows = piece.shape[0]
-        cut = (rows // 2 + 15) // 16 * 16
-        self.cuts = ((0, cut), (cut, rows - cut))
+        side = (rows // 3 + 15) // 16 * 16
+        self.cuts = ((0, side), (side, rows - 2 * side), (rows - side, side))
         self.sent = []
 
     def greet(self):
@@ -128,7 +129,7 @@
 
     def copy(self, way, slot, chip, part, own=False):
         first, count = self.cuts[part]
-        place = self.held.at[self.core, chip, pl.ds(first, count)]
+        place = self.held.at[chip, self.core, pl.ds(first, count)]
         return pltpu.make_async_remote_copy(
             src_ref=self.piece.at[pl.ds(first, count)] if own else place,
             dst_ref=place,
@@ -145,34 +146,44 @@
 
     def start(self):
         chip = self.chip(0, 0, 0)
-        self.own = pltpu.make_async_copy(self.piece, self.held.at[self.core, chip], self.own_sem)
+        self.own = pltpu.make_async_copy(self.piece, self.held.at[chip, self.core], self.own_sem)
         self.own.start()
-        for way in ("z", "x", "y", "core"):
-            for part in range(2):
+        for part in range(PARTS):
+            for way in ("z", "y"):
                 self.send(way, part, chip, part, own=True)
+        self.send("x", 0, chip, 0, own=True)
+
+    def start_rest(self):
+        chip = self.chip(0, 0, 0)
+        for part in range(1, PARTS):
+            self.send("x", part, chip, part, own=True)
+        for part in range(PARTS):
+            self.send("core", part, chip, part, own=True)
 
     def line(self, step, part):
         chip = self.chip(step, 0, 0)
-        self.copy("z", (step - 1) * 2 + part, chip, part).wait_recv()
+        self.copy("z", (step - 1) * PARTS + part, chip, part).wait_recv()
         if step < LINE - 1:
-            self.send("z", step * 2 + part, chip, part)
+            self.send("z", step * PARTS + part, chip, part)
         for way in ("x", "y"):
-            self.send(way, step * 2 + part, chip, part)
-        self.send("core", step * 8 + part, chip, part)
+            self.send(way, step * PARTS + part, chip, part)
+        self.send("core", step * 4 * PARTS + part, chip, part)
 
     def across_x(self, step, part):
         chip = self.chip(step, 1, 0)
-        self.copy("x", step * 2 + part, chip, part).wait_recv()
+        self.copy("x", step * PARTS + part, chip, part).wait_recv()
         if part == 0:
-            self.send("y", 2 * LINE + step, chip, part)
-        self.send("core", step * 8 + 2 + part, chip, part)
+            self.send("y", PARTS * LINE + step, chip, part)
+        if part == 2 and step == 0:
+            self.send("y", (PARTS + 1) * LINE, chip, part)
+        self.send("core", (step * 4 + 1) * PARTS + part, chip, part)
 
     def across_y(self, step, part):
         chip = self.chip(step, 0, 1)
-        self.copy("y", step * 2 + part, chip, part).wait_recv()
+        self.copy("y", step * PARTS + part, chip, part).wait_recv()
         if part == 1:
-            self.send("x", 2 * LINE + step, chip, part)
-        self.send("core", step * 8 + 4 + part, chip, part)
+            self.send("x", PARTS * LINE + step, chip, part)
+        self.send("core", (step * 4 + 2) * PARTS + part, chip, part)
 
     def across(self, step, part):
         self.across_x(step, part)
@@ -180,16 +191,24 @@
 
     def corner(self, step):
         chip = self.chip(step, 1, 1)
-        for part, way in enumerate(("y", "x")):
-            self.copy(way, 2 * LINE + step, chip, part).wait_recv()
-            self.send("core", step * 8 + 6 + part, chip, part)
+        ways = (
+            ("y", PARTS * LINE + step),
+            ("x", PARTS * LINE + step),
+            ("z", PARTS * (LINE - 1) + step - 1) if step else ("y", (PARTS + 1) * LINE),
+        )
+        for part in (2, 0, 1):
+            way, slot = ways[part]
+            self.copy(way, slot, chip, part).wait_recv()
+            if part == 2 and step < LINE - 1:
+                self.send("z", PARTS * (LINE - 1) + step, chip, part)
+            self.send("core", (step * 4 + 3) * PARTS + part, chip, part)
 
     def ready(self, step, kind):
         chip = self.chip(step, kind % 2, kind // 2)
-        for part in range(2):
+        for part in range(PARTS):
             first, count = self.cuts[part]
-            place = self.held.at[1 - self.core, chip, pl.ds(first, count)]
-            slot = step * 8 + kind * 2 + part
+            place = self.held.at[chip, 1 - self.core, pl.ds(first, count)]
+            slot = (step * 4 + kind) * PARTS + part
             pltpu.make_async_remote_copy(
                 src_ref=place,
                 dst_ref=place,
@@ -216,7 +235,7 @@
 
 def layer_kernel(
     x_in, gate_in, keys, queries, decay, mix, gain, piece, hidden,
-    held, x_cols, gate_cols, normed, mixed, run_col, run_row, tail, level_scale,
+    held, x_cols, gate_cols, gain_cols, normed, mixed, run_col, run_row, tail, level_scale,
     level_of, scores, state, state_out, state_in, decay_out, decay_in,
     z_sems, x_sems, y_sems, core_sems, own_sem, state_sems, decay_sems,
 ):
@@ -275,6 +294,7 @@
     rounds = [exchange(0)]
     for copy in rounds[0]:
         copy.start()
+    gather.start_rest()
 
     gather.line(1, 0)
     gather.across(0, 0)
@@ -295,6 +315,8 @@
 
     gather.line(1, 1)
     gather.across(0, 1)
+    gather.line(1, 2)
+    gather.across(0, 2)
 
     def local(head, _):
         run_t = run_row[pl.ds(head, 1), :]
@@ -373,33 +395,37 @@
         lax.fori_loop(0, heads // GROUP, add, 0)
 
     locals_of(0)
+    total, prefix = merge(0, total, prefix)
     gather.line(2, 0)
-    total, prefix = merge(0, total, prefix)
     gather.across(1, 0)
     locals_of(1)
     gather.line(2, 1)
+    gather.line(2, 2)
+    gather.corner(0)
+    locals_of(2)
     gather.across(1, 1)
-    locals_of(2)
+    gather.across(1, 2)
     gather.line(3, 0)
-    gather.corner(0)
     total, prefix = merge(1, total, prefix)
     scale_level(2, prefix)
     gather.line(3, 1)
+    gather.line(3, 2)
+    gather.corner(1)
+    locals_of(3)
     gather.across(2, 0)
-    locals_of(3)
-    gather.corner(1)
+    distant(0)
     gather.across(2, 1)
-    distant(0)
     distant(1)
+    gather.across(2, 2)
 
     def turn_gate(index, _):
         lanes = rows_of(index, 128)
         gate_cols[lanes, :] = gate_in[:, lanes].astype(f32).T.astype(bf16)
+        gain_cols[lanes, :] = jnp.broadcast_to(gain[:, lanes], (128, 128)).T
         return 0
 
     lax.fori_loop(0, gate_cols.shape[0] // 128, turn_gate, 0)
-    gather.across(3, 0)
-    gather.across(3, 1)
+    gather.corner(2)
     rounds[2][0].wait_recv()
     distant(2)
 
@@ -415,27 +441,41 @@
 
     def norm(index, _):
         rows = rows_of(index, head_dim)
-        normed[rows, :] = (mixed[rows, :] * scale * gain[rows, :]).astype(bf16)
+        gains = gain_cols[rows, :]
+        value = mixed[rows, :] * scale * jnp.concatenate([gains, gains], axis=1)
+        normed[rows, :] = value.astype(bf16)
         return 0
 
     lax.fori_loop(0, heads, norm, 0)
 
-    def project(chip):
-        gate = jnp.dot(held[0, chip], normed[...], preferred_element_type=f32)
-        up = jnp.dot(held[1, chip], normed[...], preferred_element_type=f32)
-        hidden[chip] = (gate / (1.0 + jnp.exp(-gate)) * up).astype(bf16)
+    rows = piece.shape[0]
+
+    def project(chip, count):
+        weights = held[pl.ds(chip, count)].reshape(count * 2 * rows, held.shape[3])
+        both = jnp.dot(weights, normed[...], preferred_element_type=f32)
+        both = both.reshape(count, 2, rows, SPAN)
+        gate, up = both[:, 0], both[:, 1]
+        hidden[pl.ds(chip, count)] = (gate / (1.0 + jnp.exp(-gate)) * up).astype(bf16)
+
+    def project_pair(step, kind):
+        chip = gather.ready(step, kind)
+        gather.ready(step, kind + 2)
+        project(chip // 2 * 2, 2)
 
     gather.own.wait()
-    for step in range(LINE - 1):
-        for kind in range(4):
-            if (step, kind) != (2, 3):
-                project(gather.ready(step, kind))
-    gather.corner(2)
-    for kind in range(3):
-        project(gather.ready(3, kind))
-    project(gather.ready(2, 3))
+    project_pair(0, 0)
+    project_pair(0, 1)
+    gather.across(3, 0)
+    gather.across(3, 1)
+    project_pair(1, 0)
+    gather.across(3, 2)
+    project_pair(1, 1)
+    project_pair(2, 0)
+    project_pair(2, 1)
+    project_pair(3, 0)
+    project(gather.ready(3, 1), 1)
     gather.corner(3)
-    project(gather.ready(3, 3))
+    project(gather.ready(3, 3), 1)
     gather.finish()
     for copies in rounds:
         for copy in copies:
@@ -464,9 +504,10 @@
         in_specs=[pl.BlockSpec(memory_space=pltpu.VMEM)] * 8,
         out_specs=pl.BlockSpec(memory_space=pltpu.VMEM),
         scratch_shapes=[
-            pltpu.VMEM((2, CHIPS, rows, depth), bf16),
+            pltpu.VMEM((CHIPS, 2, rows, depth), bf16),
             pltpu.VMEM((depth, tokens), bf16),
             pltpu.VMEM((depth, tokens), bf16),
+            pltpu.VMEM((depth, 128), f32),
             pltpu.VMEM((depth, tokens), bf16),
             pltpu.VMEM((depth, tokens), f32),
             pltpu.VMEM((heads, tokens, 128), f32),
@@ -480,10 +521,10 @@
             pltpu.VMEM((3, depth, states), bf16),
             pltpu.VMEM((2, heads, 128), f32),
             pltpu.VMEM((2, heads, 128), f32),
-            sems((2, 6)),
-            sems((2, 12)),
-            sems((2, 12)),
-            sems((2, 2 * CHIPS)),
+            sems((2, (PARTS + 1) * (LINE - 1))),
+            sems((2, (PARTS + 1) * LINE)),
+            sems((2, (PARTS + 1) * LINE + 1)),
+            sems((2, PARTS * CHIPS)),
             sems,
             sems((2, 3)),
             sems((2, 2)),
@@ -496,7 +537,7 @@
             bytes_accessed=2 * CHIPS * rows * depth * 2,
             transcendentals=tokens * CHIPS * rows,
         ),
-    )(x, gate, keys, queries, decay, mix, norm_gain[:, None], piece)
+    )(x, gate, keys, queries, decay, mix, norm_gain[None, :], piece)
     return hidden.reshape(CHIPS * rows, tokens).T
 
 

time: 123 us -> 137 us (1.11)
  Pallas kernels: 116 us -> 128 us
  local copies, waits for them, and re-layouts: 4.58 us -> 2.53 us
    pallas_call x1, Pallas kernels: 116 us -> 128 us  [streamed_layer(): pl.pallas_call(layer_kernel, out_shape=jax.ShapeDtypeStruct((CHIPS, rows,...]
    broadcast_in_dim x1 -> x0, local copies, waits for them, and re-layouts: 2.04 us -> none  [streamed_layer(): norm_gain[:, None]]
  transfers between devices with their start and end apart: 1 -> 1, of which waited for: 0 -> 1; matrix products, arithmetic and copies ran while one was open for 2% -> 0% of each run, Pallas kernels for 0% -> 0%
where the time goes in v3:
time: 137 us; the launch traced here: 136 us
  Pallas kernels  128 us (93%)
  other arithmetic  3.25 us (2%)
  local copies, waits for them, and re-layouts  2.53 us (2%)
    pallas_call x1, Pallas kernels, streamed_layer(): pl.pallas_call(layer_kernel, out_shape=jax.ShapeDtypeStruct((CHIPS, rows,...  128 us
  transfers between devices with their start and end apart: 1, of which 1 were waited for; matrix products, arithmetic and copies ran while one was open for 0% of the time, Pallas kernels for 0%

profile of v3, /device:TPU:0, one launch (start us, length us, event | category | flops | bytes accessed | tf_op | source)
XLA Modules:
  0.0 136.1 jit_solution(11271048555019148837)
XLA Ops:
  0.0 1.1 broadcast_select_fusion
  1.1 0.5 collective-permute-start
  1.7 1.3 collective-permute-done
  3.0 2.1 %maximum_select_fusion.piece = bf16[176,2048]{1,0:T(8,128)(2,1)} fusion(bf16[88,2048]{1,0:T(8,128)(2,1)S(1)} %collective-permute-done, bf16[88,2048]{1,0:T(8,128)(2,1)} %bitcast.17, bf16[88,2048]{1,0:T(8,128)(2,1)} %bitcast.16, pred[]{:T(512)S(6)} %eq.5), kind=kLoop, calls=%fused_computation | loop fusion | flops 3244032 | bytes 1802241 | tf_op jit(solution)/shard_map/jit(_where)/select_n | solution.py:490
  5.1 128.4 %shard_map.91 = bf16[16,176,256]{2,1,0:T(8,128)(2,1)} custom-call(bf16[256,2048]{1,0:T(8,128)(2,1)} %bitcast.18, bf16[256,2048]{1,0:T(8,128)(2,1)} %bitcast.19, bf16[256,128]{1,0:T(8,128)(2,1)} %bitcast.21, bf16[256,128]{1,0:T(8,128)(2,1)} %bitcast.22, f32[32,256]{1,0:T(8,128)} %bitcast.23, f32[12,32,256]{2,1,0:T(8,128)} %bitcast.20, f32[1,2048]{1,0:T(1,128)} %bitcast.24, ...), custom_call_target="tpu_custom_call" | custom-call | flops 5905580032 | bytes 23068672 | tf_op jit(solution)/shard_map/pallas_call | solution.py:501
  133.5 2.5 %copy.10 = bf16[2816,256]{0,1:T(8,128)(2,1)} copy(bf16[2816,256]{1,0:T(8,128)(2,1)} %bitcast.15) | data formatting | bytes 2883584 | tf_op jit(solution)/shard_map/reshape | solution.py:541
Async XLA Ops:
  1.1 1.8 %collective-permute-start = (bf16[88,2048]{1,0:T(8,128)(2,1)S(1)}, bf16[88,2048]{1,0:T(8,128)(2,1)S(1)}, u32[]{:S(2)}, u32[]{:S(2)}) collective-permute-start(bf16[88,2048]{1,0:T(8,128)(2,1)S(1)} %broadcast_select_fusion), channel_id=1, source_target_pairs={{0,1},{1,0},{2,3},{3,2},{4,5},{5,4},{6,7},{7,6},{8,9},{9,8},{10,11... | collective-permute-start | bytes 1081352 | tf_op jit(solution)/shard_map/ppermute | solution.py:489

commit v4 on v2

--- a/solution.py
+++ b/solution.py
@@ -147,9 +147,16 @@
         chip = self.chip(0, 0, 0)
         self.own = pltpu.make_async_copy(self.piece, self.held.at[self.core, chip], self.own_sem)
         self.own.start()
-        for way in ("z", "x", "y", "core"):
-            for part in range(2):
+        for part in range(2):
+            for way in ("z", "y"):
                 self.send(way, part, chip, part, own=True)
+        self.send("x", 0, chip, 0, own=True)
+
+    def start_rest(self):
+        chip = self.chip(0, 0, 0)
+        self.send("x", 1, chip, 1, own=True)
+        for part in range(2):
+            self.send("core", part, chip, part, own=True)
 
     def line(self, step, part):
         chip = self.chip(step, 0, 0)
@@ -216,7 +223,7 @@
 
 def layer_kernel(
     x_in, gate_in, keys, queries, decay, mix, gain, piece, hidden,
-    held, x_cols, gate_cols, normed, mixed, run_col, run_row, tail, level_scale,
+    held, x_cols, gate_cols, gain_cols, normed, mixed, run_col, run_row, tail, level_scale,
     level_of, scores, state, state_out, state_in, decay_out, decay_in,
     z_sems, x_sems, y_sems, core_sems, own_sem, state_sems, decay_sems,
 ):
@@ -275,6 +282,7 @@
     rounds = [exchange(0)]
     for copy in rounds[0]:
         copy.start()
+    gather.start_rest()
 
     gather.line(1, 0)
     gather.across(0, 0)
@@ -373,33 +381,32 @@
         lax.fori_loop(0, heads // GROUP, add, 0)
 
     locals_of(0)
+    total, prefix = merge(0, total, prefix)
     gather.line(2, 0)
-    total, prefix = merge(0, total, prefix)
     gather.across(1, 0)
     locals_of(1)
     gather.line(2, 1)
     gather.across(1, 1)
     locals_of(2)
+    total, prefix = merge(1, total, prefix)
+    scale_level(2, prefix)
     gather.line(3, 0)
     gather.corner(0)
-    total, prefix = merge(1, total, prefix)
-    scale_level(2, prefix)
+    locals_of(3)
     gather.line(3, 1)
+    distant(0)
     gather.across(2, 0)
-    locals_of(3)
+    distant(1)
     gather.corner(1)
-    gather.across(2, 1)
-    distant(0)
-    distant(1)
 
     def turn_gate(index, _):
         lanes = rows_of(index, 128)
         gate_cols[lanes, :] = gate_in[:, lanes].astype(f32).T.astype(bf16)
+        gain_cols[lanes, :] = jnp.broadcast_to(gain[:, lanes], (128, 128)).T
         return 0
 
     lax.fori_loop(0, gate_cols.shape[0] // 128, turn_gate, 0)
-    gather.across(3, 0)
-    gather.across(3, 1)
+    gather.across(2, 1)
     rounds[2][0].wait_recv()
     distant(2)
 
@@ -415,7 +422,9 @@
 
     def norm(index, _):
         rows = rows_of(index, head_dim)
-        normed[rows, :] = (mixed[rows, :] * scale * gain[rows, :]).astype(bf16)
+        gains = gain_cols[rows, :]
+        value = mixed[rows, :] * scale * jnp.concatenate([gains, gains], axis=1)
+        normed[rows, :] = value.astype(bf16)
         return 0
 
     lax.fori_loop(0, heads, norm, 0)
@@ -426,14 +435,18 @@
         hidden[chip] = (gate / (1.0 + jnp.exp(-gate)) * up).astype(bf16)
 
     gather.own.wait()
-    for step in range(LINE - 1):
-        for kind in range(4):
-            if (step, kind) != (2, 3):
-                project(gather.ready(step, kind))
+    for kind in range(4):
+        project(gather.ready(0, kind))
+    gather.across(3, 0)
+    for kind in range(4):
+        project(gather.ready(1, kind))
+    gather.across(3, 1)
+    for kind in range(3):
+        project(gather.ready(2, kind))
     gather.corner(2)
+    project(gather.ready(2, 3))
     for kind in range(3):
         project(gather.ready(3, kind))
-    project(gather.ready(2, 3))
     gather.corner(3)
     project(gather.ready(3, 3))
     gather.finish()
@@ -467,6 +480,7 @@
             pltpu.VMEM((2, CHIPS, rows, depth), bf16),
             pltpu.VMEM((depth, tokens), bf16),
             pltpu.VMEM((depth, tokens), bf16),
+            pltpu.VMEM((depth, 128), f32),
             pltpu.VMEM((depth, tokens), bf16),
             pltpu.VMEM((depth, tokens), f32),
             pltpu.VMEM((heads, tokens, 128), f32),
@@ -496,7 +510,7 @@
             bytes_accessed=2 * CHIPS * rows * depth * 2,
             transcendentals=tokens * CHIPS * rows,
         ),
-    )(x, gate, keys, queries, decay, mix, norm_gain[:, None], piece)
+    )(x, gate, keys, queries, decay, mix, norm_gain[None, :], piece)
     return hidden.reshape(CHIPS * rows, tokens).T
 
 

time: 123 us -> 126 us (1.024); the launches traced: 123 us -> 125 us
  local copies, waits for them, and re-layouts: 4.58 us -> 2.53 us
  waiting for transfers between devices: 0.01 us -> 1.3 us
    broadcast_in_dim x1 -> x0, local copies, waits for them, and re-layouts: 2.04 us -> none  [streamed_layer(): norm_gain[:, None]]
    pallas_call x1, Pallas kernels: 116 us -> 117 us  [streamed_layer(): pl.pallas_call(layer_kernel, out_shape=jax.ShapeDtypeStruct((CHIPS, rows,...]
    ppermute x1, waiting for transfers between devices: 0.01 us -> 1.3 us  [chip_rows(): other = lax.ppermute(jnp.where(first, up, gate), 'dp', pairs)]
  transfers between devices with their start and end apart: 1 -> 1, of which waited for: 0 -> 1; matrix products, arithmetic and copies ran while one was open for 2% -> 0% of each run, Pallas kernels for 0% -> 0%
where the time goes in v4:
time: 126 us; the launch traced here: 125 us
  Pallas kernels  117 us (93%)
  other arithmetic  3.25 us (3%)
  local copies, waits for them, and re-layouts  2.53 us (2%)
  waiting for transfers between devices  1.3 us (1%)
    pallas_call x1, Pallas kernels, streamed_layer(): pl.pallas_call(layer_kernel, out_shape=jax.ShapeDtypeStruct((CHIPS, rows,...  117 us
    reshape x1, local copies, waits for them, and re-layouts, streamed_layer(): return hidden.reshape(CHIPS * rows, tokens).T  2.53 us
  transfers between devices with their start and end apart: 1, of which 1 were waited for; matrix products, arithmetic and copies ran while one was open for 0% of the time, Pallas kernels for 0%

profile of v4, /device:TPU:0, one launch (start us, length us, event | category | flops | bytes accessed | tf_op | source)
XLA Modules:
  0.0 124.9 jit_solution(13080283131079850250)
XLA Ops:
  0.0 1.1 broadcast_select_fusion
  1.1 0.5 collective-permute-start
  1.7 1.3 %collective-permute-done = bf16[88,2048]{1,0:T(8,128)(2,1)S(1)} collective-permute-done((bf16[88,2048]{1,0:T(8,128)(2,1)S(1)}, bf16[88,2048]{1,0:T(8,128)(2,1)S(1)}, u32[]{:S(2)}, u32[]{:S(2)}) %collective-permute-start) | collective-permute-done | bytes 360480 | tf_op jit(solution)/shard_map/ppermute | solution.py:462
  3.0 2.1 %maximum_select_fusion.piece = bf16[176,2048]{1,0:T(8,128)(2,1)} fusion(bf16[88,2048]{1,0:T(8,128)(2,1)S(1)} %collective-permute-done, bf16[88,2048]{1,0:T(8,128)(2,1)} %bitcast.17, bf16[88,2048]{1,0:T(8,128)(2,1)} %bitcast.16, pred[]{:T(512)S(6)} %eq.5), kind=kLoop, calls=%fused_computation | loop fusion | flops 3244032 | bytes 1802241 | tf_op jit(solution)/shard_map/jit(_where)/select_n | solution.py:463
  5.1 117.3 %shard_map.91 = bf16[16,176,256]{2,1,0:T(8,128)(2,1)} custom-call(bf16[256,2048]{1,0:T(8,128)(2,1)} %bitcast.18, bf16[256,2048]{1,0:T(8,128)(2,1)} %bitcast.19, bf16[256,128]{1,0:T(8,128)(2,1)} %bitcast.21, bf16[256,128]{1,0:T(8,128)(2,1)} %bitcast.22, f32[32,256]{1,0:T(8,128)} %bitcast.23, f32[12,32,256]{2,1,0:T(8,128)} %bitcast.20, f32[1,2048]{1,0:T(1,128)} %bitcast.24, ...), custom_call_target="tpu_custom_call" | custom-call | flops 5905580032 | bytes 23068672 | tf_op jit(solution)/shard_map/pallas_call | solution.py:474
  122.4 2.5 %copy.10 = bf16[2816,256]{0,1:T(8,128)(2,1)} copy(bf16[2816,256]{1,0:T(8,128)(2,1)} %bitcast.15) | data formatting | bytes 2883584 | tf_op jit(solution)/shard_map/reshape | solution.py:514
Async XLA Ops:
  1.1 1.8 %collective-permute-start = (bf16[88,2048]{1,0:T(8,128)(2,1)S(1)}, bf16[88,2048]{1,0:T(8,128)(2,1)S(1)}, u32[]{:S(2)}, u32[]{:S(2)}) collective-permute-start(bf16[88,2048]{1,0:T(8,128)(2,1)S(1)} %broadcast_select_fusion), channel_id=1, source_target_pairs={{0,1},{1,0},{2,3},{3,2},{4,5},{5,4},{6,7},{7,6},{8,9},{9,8},{10,11... | collective-permute-start | bytes 1081352 | tf_op jit(solution)/shard_map/ppermute | solution.py:462

commit v5 on v3

--- a/solution.py
+++ b/solution.py
@@ -191,17 +191,20 @@
 
     def corner(self, step):
         chip = self.chip(step, 1, 1)
-        ways = (
-            ("y", PARTS * LINE + step),
-            ("x", PARTS * LINE + step),
-            ("z", PARTS * (LINE - 1) + step - 1) if step else ("y", (PARTS + 1) * LINE),
-        )
-        for part in (2, 0, 1):
-            way, slot = ways[part]
-            self.copy(way, slot, chip, part).wait_recv()
-            if part == 2 and step < LINE - 1:
-                self.send("z", PARTS * (LINE - 1) + step, chip, part)
+        for part, way in enumerate(("y", "x")):
+            self.copy(way, PARTS * LINE + step, chip, part).wait_recv()
             self.send("core", (step * 4 + 3) * PARTS + part, chip, part)
+
+    def corner_line(self, step):
+        chip, part = self.chip(step, 1, 1), 2
+        if step:
+            way, slot = "z", PARTS * (LINE - 1) + step - 1
+        else:
+            way, slot = "y", (PARTS + 1) * LINE
+        self.copy(way, slot, chip, part).wait_recv()
+        if step < LINE - 1:
+            self.send("z", PARTS * (LINE - 1) + step, chip, part)
+        self.send("core", (step * 4 + 3) * PARTS + part, chip, part)
 
     def ready(self, step, kind):
         chip = self.chip(step, kind % 2, kind // 2)
@@ -394,40 +397,43 @@
 
         lax.fori_loop(0, heads // GROUP, add, 0)
 
+    def turn_gate(index, _):
+        lanes = rows_of(index, 128)
+        gate_cols[lanes, :] = gate_in[:, lanes].astype(f32).T.astype(bf16)
+        gain_cols[lanes, :] = jnp.broadcast_to(gain[:, lanes], (128, 128)).T
+        return 0
+
+    lax.fori_loop(0, gate_cols.shape[0] // 128, turn_gate, 0)
+    total, prefix = merge(0, total, prefix)
     locals_of(0)
-    total, prefix = merge(0, total, prefix)
     gather.line(2, 0)
     gather.across(1, 0)
     locals_of(1)
     gather.line(2, 1)
     gather.line(2, 2)
-    gather.corner(0)
-    locals_of(2)
     gather.across(1, 1)
     gather.across(1, 2)
-    gather.line(3, 0)
     total, prefix = merge(1, total, prefix)
     scale_level(2, prefix)
+    gather.line(3, 0)
     gather.line(3, 1)
     gather.line(3, 2)
+    locals_of(2)
+    gather.corner(0)
+    gather.across(2, 0)
+    locals_of(3)
+    gather.across(2, 1)
+    distant(0)
+    gather.across(2, 2)
+    distant(1)
     gather.corner(1)
-    locals_of(3)
-    gather.across(2, 0)
-    distant(0)
-    gather.across(2, 1)
-    distant(1)
-    gather.across(2, 2)
-
-    def turn_gate(index, _):
-        lanes = rows_of(index, 128)
-        gate_cols[lanes, :] = gate_in[:, lanes].astype(f32).T.astype(bf16)
-        gain_cols[lanes, :] = jnp.broadcast_to(gain[:, lanes], (128, 128)).T
-        return 0
-
-    lax.fori_loop(0, gate_cols.shape[0] // 128, turn_gate, 0)
-    gather.corner(2)
+    gather.across(3, 0)
+    gather.across(3, 1)
+    gather.across(3, 2)
+    gather.corner_line(0)
     rounds[2][0].wait_recv()
     distant(2)
+    gather.corner_line(1)
 
     def gated(index, squares):
         rows = rows_of(index, head_dim)
@@ -439,6 +445,8 @@
     squares = lax.fori_loop(0, heads, gated, jnp.zeros((1, SPAN), f32))
     scale = lax.rsqrt(squares / mixed.shape[0] + EPS)
 
+    gather.corner_line(2)
+
     def norm(index, _):
         rows = rows_of(index, head_dim)
         gains = gain_cols[rows, :]
@@ -450,32 +458,24 @@
 
     rows = piece.shape[0]
 
-    def project(chip, count):
-        weights = held[pl.ds(chip, count)].reshape(count * 2 * rows, held.shape[3])
+    def project(chip):
+        weights = held[chip].reshape(2 * rows, held.shape[3])
         both = jnp.dot(weights, normed[...], preferred_element_type=f32)
-        both = both.reshape(count, 2, rows, SPAN)
-        gate, up = both[:, 0], both[:, 1]
-        hidden[pl.ds(chip, count)] = (gate / (1.0 + jnp.exp(-gate)) * up).astype(bf16)
-
-    def project_pair(step, kind):
-        chip = gather.ready(step, kind)
-        gather.ready(step, kind + 2)
-        project(chip // 2 * 2, 2)
+        gate, up = both[:rows], both[rows:]
+        hidden[chip] = (gate / (1.0 + jnp.exp(-gate)) * up).astype(bf16)
 
     gather.own.wait()
-    project_pair(0, 0)
-    project_pair(0, 1)
-    gather.across(3, 0)
-    gather.across(3, 1)
-    project_pair(1, 0)
-    gather.across(3, 2)
-    project_pair(1, 1)
-    project_pair(2, 0)
-    project_pair(2, 1)
-    project_pair(3, 0)
-    project(gather.ready(3, 1), 1)
+    for step in range(2):
+        for kind in range(4):
+            project(gather.ready(step, kind))
+    gather.corner(2)
+    for kind in range(4):
+        project(gather.ready(2, kind))
+    for kind in range(3):
+        project(gather.ready(3, kind))
+    gather.corner_line(3)
     gather.corner(3)
-    project(gather.ready(3, 3), 1)
+    project(gather.ready(3, 3))
     gather.finish()
     for copies in rounds:
         for copy in copies:

time: 137 us -> 141 us (1.029)
  Pallas kernels: 128 us -> 132 us
    pallas_call x1, Pallas kernels: 128 us -> 132 us  [streamed_layer(): pl.pallas_call(layer_kernel, out_shape=jax.ShapeDtypeStruct((CHIPS, rows,...]
where the time goes in v5:
time: 141 us; the launch traced here: 140 us
  Pallas kernels  132 us (94%)
  other arithmetic  3.25 us (2%)
  local copies, waits for them, and re-layouts  2.53 us (2%)
    pallas_call x1, Pallas kernels, streamed_layer(): pl.pallas_call(layer_kernel, out_shape=jax.ShapeDtypeStruct((CHIPS, rows,...  132 us
  transfers between devices with their start and end apart: 1, of which 1 were waited for; matrix products, arithmetic and copies ran while one was open for 0% of the time, Pallas kernels for 0%

profile of v5, /device:TPU:0, one launch (start us, length us, event | category | flops | bytes accessed | tf_op | source)
XLA Modules:
  0.0 140.0 jit_solution(12003642232966513426)
XLA Ops:
  0.0 1.1 broadcast_select_fusion
  1.1 0.5 collective-permute-start
  1.7 1.3 collective-permute-done
  3.0 2.1 %maximum_select_fusion.piece = bf16[176,2048]{1,0:T(8,128)(2,1)} fusion(bf16[88,2048]{1,0:T(8,128)(2,1)S(1)} %collective-permute-done, bf16[88,2048]{1,0:T(8,128)(2,1)} %bitcast.17, bf16[88,2048]{1,0:T(8,128)(2,1)} %bitcast.16, pred[]{:T(512)S(6)} %eq.5), kind=kLoop, calls=%fused_computation | loop fusion | flops 3244032 | bytes 1802241 | tf_op jit(solution)/shard_map/jit(_where)/select_n | solution.py:490
  5.1 132.4 %shard_map.91 = bf16[16,176,256]{2,1,0:T(8,128)(2,1)} custom-call(bf16[256,2048]{1,0:T(8,128)(2,1)} %bitcast.18, bf16[256,2048]{1,0:T(8,128)(2,1)} %bitcast.19, bf16[256,128]{1,0:T(8,128)(2,1)} %bitcast.21, bf16[256,128]{1,0:T(8,128)(2,1)} %bitcast.22, f32[32,256]{1,0:T(8,128)} %bitcast.23, f32[12,32,256]{2,1,0:T(8,128)} %bitcast.20, f32[1,2048]{1,0:T(1,128)} %bitcast.24, ...), custom_call_target="tpu_custom_call" | custom-call | flops 5905580032 | bytes 23068672 | tf_op jit(solution)/shard_map/pallas_call | solution.py:501
  137.5 2.5 %copy.10 = bf16[2816,256]{0,1:T(8,128)(2,1)} copy(bf16[2816,256]{1,0:T(8,128)(2,1)} %bitcast.15) | data formatting | bytes 2883584 | tf_op jit(solution)/shard_map/reshape | solution.py:541
Async XLA Ops:
  1.1 1.8 %collective-permute-start = (bf16[88,2048]{1,0:T(8,128)(2,1)S(1)}, bf16[88,2048]{1,0:T(8,128)(2,1)S(1)}, u32[]{:S(2)}, u32[]{:S(2)}) collective-permute-start(bf16[88,2048]{1,0:T(8,128)(2,1)S(1)} %broadcast_select_fusion), channel_id=1, source_target_pairs={{0,1},{1,0},{2,3},{3,2},{4,5},{5,4},{6,7},{7,6},{8,9},{9,8},{10,11... | collective-permute-start | bytes 1081352 | tf_op jit(solution)/shard_map/ppermute | solution.py:489

commit v6 on v4

--- a/solution.py
+++ b/solution.py
@@ -128,7 +128,7 @@
 
     def copy(self, way, slot, chip, part, own=False):
         first, count = self.cuts[part]
-        place = self.held.at[self.core, chip, pl.ds(first, count)]
+        place = self.held.at[chip, self.core, pl.ds(first, count)]
         return pltpu.make_async_remote_copy(
             src_ref=self.piece.at[pl.ds(first, count)] if own else place,
             dst_ref=place,
@@ -145,7 +145,7 @@
 
     def start(self):
         chip = self.chip(0, 0, 0)
-        self.own = pltpu.make_async_copy(self.piece, self.held.at[self.core, chip], self.own_sem)
+        self.own = pltpu.make_async_copy(self.piece, self.held.at[chip, self.core], self.own_sem)
         self.own.start()
         for part in range(2):
             for way in ("z", "y"):
@@ -195,7 +195,7 @@
         chip = self.chip(step, kind % 2, kind // 2)
         for part in range(2):
             first, count = self.cuts[part]
-            place = self.held.at[1 - self.core, chip, pl.ds(first, count)]
+            place = self.held.at[chip, 1 - self.core, pl.ds(first, count)]
             slot = step * 8 + kind * 2 + part
             pltpu.make_async_remote_copy(
                 src_ref=place,
@@ -380,22 +380,23 @@
 
         lax.fori_loop(0, heads // GROUP, add, 0)
 
+    total, prefix = merge(0, total, prefix)
     locals_of(0)
-    total, prefix = merge(0, total, prefix)
     gather.line(2, 0)
     gather.across(1, 0)
     locals_of(1)
     gather.line(2, 1)
     gather.across(1, 1)
-    locals_of(2)
     total, prefix = merge(1, total, prefix)
     scale_level(2, prefix)
     gather.line(3, 0)
     gather.corner(0)
+    locals_of(2)
+    gather.line(3, 1)
+    gather.across(2, 0)
     locals_of(3)
-    gather.line(3, 1)
     distant(0)
-    gather.across(2, 0)
+    gather.across(2, 1)
     distant(1)
     gather.corner(1)
 
@@ -406,7 +407,8 @@
         return 0
 
     lax.fori_loop(0, gate_cols.shape[0] // 128, turn_gate, 0)
-    gather.across(2, 1)
+    gather.across(3, 0)
+    gather.across(3, 1)
     rounds[2][0].wait_recv()
     distant(2)
 
@@ -429,26 +431,27 @@
 
     lax.fori_loop(0, heads, norm, 0)
 
-    def project(chip):
-        gate = jnp.dot(held[0, chip], normed[...], preferred_element_type=f32)
-        up = jnp.dot(held[1, chip], normed[...], preferred_element_type=f32)
-        hidden[chip] = (gate / (1.0 + jnp.exp(-gate)) * up).astype(bf16)
+    rows = piece.shape[0]
+
+    def project_pair(step, kind):
+        chip = gather.ready(step, kind) // 2 * 2
+        gather.ready(step, kind + 2)
+        weights = held[pl.ds(chip, 2)].reshape(4 * rows, held.shape[3])
+        both = jnp.dot(weights, normed[...], preferred_element_type=f32)
+        both = both.reshape(2, 2, rows, SPAN)
+        gate, up = both[:, 0], both[:, 1]
+        hidden[pl.ds(chip, 2)] = (gate / (1.0 + jnp.exp(-gate)) * up).astype(bf16)
 
     gather.own.wait()
-    for kind in range(4):
-        project(gather.ready(0, kind))
-    gather.across(3, 0)
-    for kind in range(4):
-        project(gather.ready(1, kind))
-    gather.across(3, 1)
-    for kind in range(3):
-        project(gather.ready(2, kind))
+    for step in range(2):
+        project_pair(step, 0)
+        project_pair(step, 1)
     gather.corner(2)
-    project(gather.ready(2, 3))
-    for kind in range(3):
-        project(gather.ready(3, kind))
+    project_pair(2, 0)
+    project_pair(2, 1)
+    project_pair(3, 0)
     gather.corner(3)
-    project(gather.ready(3, 3))
+    project_pair(3, 1)
     gather.finish()
     for copies in rounds:
         for copy in copies:
@@ -477,7 +480,7 @@
         in_specs=[pl.BlockSpec(memory_space=pltpu.VMEM)] * 8,
         out_specs=pl.BlockSpec(memory_space=pltpu.VMEM),
         scratch_shapes=[
-            pltpu.VMEM((2, CHIPS, rows, depth), bf16),
+            pltpu.VMEM((CHIPS, 2, rows, depth), bf16),
             pltpu.VMEM((depth, tokens), bf16),
             pltpu.VMEM((depth, tokens), bf16),
             pltpu.VMEM((depth, 128), f32),

time: 126 us -> 126 us (level)
  no operation moved by 1% of the time
where the time goes in v6:
time: 126 us; the launch traced here: 125 us
  Pallas kernels  118 us (94%)
  other arithmetic  3.25 us (3%)
  local copies, waits for them, and re-layouts  2.53 us (2%)
  waiting for transfers between devices  1.3 us (1%)
    pallas_call x1, Pallas kernels, streamed_layer(): pl.pallas_call(layer_kernel, out_shape=jax.ShapeDtypeStruct((CHIPS, rows,...  118 us
    reshape x1, local copies, waits for them, and re-layouts, streamed_layer(): return hidden.reshape(CHIPS * rows, tokens).T  2.53 us
  transfers between devices with their start and end apart: 1, of which 1 were waited for; matrix products, arithmetic and copies ran while one was open for 0% of the time, Pallas kernels for 0%

profile of v6, /device:TPU:0, one launch (start us, length us, event | category | flops | bytes accessed | tf_op | source)
XLA Modules:
  0.0 125.4 jit_solution(5082166617347926637)
XLA Ops:
  0.0 1.1 broadcast_select_fusion
  1.1 0.5 collective-permute-start
  1.7 1.3 %collective-permute-done = bf16[88,2048]{1,0:T(8,128)(2,1)S(1)} collective-permute-done((bf16[88,2048]{1,0:T(8,128)(2,1)S(1)}, bf16[88,2048]{1,0:T(8,128)(2,1)S(1)}, u32[]{:S(2)}, u32[]{:S(2)}) %collective-permute-start) | collective-permute-done | bytes 360480 | tf_op jit(solution)/shard_map/ppermute | solution.py:465
  3.0 2.1 %maximum_select_fusion.piece = bf16[176,2048]{1,0:T(8,128)(2,1)} fusion(bf16[88,2048]{1,0:T(8,128)(2,1)S(1)} %collective-permute-done, bf16[88,2048]{1,0:T(8,128)(2,1)} %bitcast.17, bf16[88,2048]{1,0:T(8,128)(2,1)} %bitcast.16, pred[]{:T(512)S(6)} %eq.5), kind=kLoop, calls=%fused_computation | loop fusion | flops 3244032 | bytes 1802241 | tf_op jit(solution)/shard_map/jit(_where)/select_n | solution.py:466
  5.1 117.8 %shard_map.91 = bf16[16,176,256]{2,1,0:T(8,128)(2,1)} custom-call(bf16[256,2048]{1,0:T(8,128)(2,1)} %bitcast.18, bf16[256,2048]{1,0:T(8,128)(2,1)} %bitcast.19, bf16[256,128]{1,0:T(8,128)(2,1)} %bitcast.21, bf16[256,128]{1,0:T(8,128)(2,1)} %bitcast.22, f32[32,256]{1,0:T(8,128)} %bitcast.23, f32[12,32,256]{2,1,0:T(8,128)} %bitcast.20, f32[1,2048]{1,0:T(1,128)} %bitcast.24, ...), custom_call_target="tpu_custom_call" | custom-call | flops 5905580032 | bytes 23068672 | tf_op jit(solution)/shard_map/pallas_call | solution.py:477
  122.8 2.5 %copy.10 = bf16[2816,256]{0,1:T(8,128)(2,1)} copy(bf16[2816,256]{1,0:T(8,128)(2,1)} %bitcast.15) | data formatting | bytes 2883584 | tf_op jit(solution)/shard_map/reshape | solution.py:517
Async XLA Ops:
  1.1 1.8 %collective-permute-start = (bf16[88,2048]{1,0:T(8,128)(2,1)S(1)}, bf16[88,2048]{1,0:T(8,128)(2,1)S(1)}, u32[]{:S(2)}, u32[]{:S(2)}) collective-permute-start(bf16[88,2048]{1,0:T(8,128)(2,1)S(1)} %broadcast_select_fusion), channel_id=1, source_target_pairs={{0,1},{1,0},{2,3},{3,2},{4,5},{5,4},{6,7},{7,6},{8,9},{9,8},{10,11... | collective-permute-start | bytes 1081352 | tf_op jit(solution)/shard_map/ppermute | solution.py:465

commit v7 on v6

--- a/solution.py
+++ b/solution.py
@@ -147,16 +147,9 @@
         chip = self.chip(0, 0, 0)
         self.own = pltpu.make_async_copy(self.piece, self.held.at[chip, self.core], self.own_sem)
         self.own.start()
-        for part in range(2):
-            for way in ("z", "y"):
+        for way in ("z", "x", "y", "core"):
+            for part in range(2):
                 self.send(way, part, chip, part, own=True)
-        self.send("x", 0, chip, 0, own=True)
-
-    def start_rest(self):
-        chip = self.chip(0, 0, 0)
-        self.send("x", 1, chip, 1, own=True)
-        for part in range(2):
-            self.send("core", part, chip, part, own=True)
 
     def line(self, step, part):
         chip = self.chip(step, 0, 0)
@@ -282,7 +275,6 @@
     rounds = [exchange(0)]
     for copy in rounds[0]:
         copy.start()
-    gather.start_rest()
 
     gather.line(1, 0)
     gather.across(0, 0)
@@ -380,25 +372,25 @@
 
         lax.fori_loop(0, heads // GROUP, add, 0)
 
-    total, prefix = merge(0, total, prefix)
     locals_of(0)
     gather.line(2, 0)
+    total, prefix = merge(0, total, prefix)
     gather.across(1, 0)
     locals_of(1)
     gather.line(2, 1)
     gather.across(1, 1)
+    locals_of(2)
+    gather.line(3, 0)
+    gather.corner(0)
     total, prefix = merge(1, total, prefix)
     scale_level(2, prefix)
-    gather.line(3, 0)
-    gather.corner(0)
-    locals_of(2)
     gather.line(3, 1)
     gather.across(2, 0)
     locals_of(3)
+    gather.corner(1)
+    gather.across(2, 1)
     distant(0)
-    gather.across(2, 1)
     distant(1)
-    gather.corner(1)
 
     def turn_gate(index, _):
         lanes = rows_of(index, 128)

time: 126 us -> 126 us (level)
  no operation moved by 1% of the time
where the time goes in v7:
time: 126 us; the launch traced here: 125 us
  Pallas kernels  118 us (94%)
  other arithmetic  3.25 us (3%)
  local copies, waits for them, and re-layouts  2.53 us (2%)
  waiting for transfers between devices  1.3 us (1%)
    pallas_call x1, Pallas kernels, streamed_layer(): pl.pallas_call(layer_kernel, out_shape=jax.ShapeDtypeStruct((CHIPS, rows,...  118 us
    reshape x1, local copies, waits for them, and re-layouts, streamed_layer(): return hidden.reshape(CHIPS * rows, tokens).T  2.53 us
  transfers between devices with their start and end apart: 1, of which 1 were waited for; matrix products, arithmetic and copies ran while one was open for 0% of the time, Pallas kernels for 0%

profile of v7, /device:TPU:0, one launch (start us, length us, event | category | flops | bytes accessed | tf_op | source)
XLA Modules:
  0.0 125.4 jit_solution(11161659660214474362)
XLA Ops:
  0.0 1.1 broadcast_select_fusion
  1.1 0.5 collective-permute-start
  1.7 1.3 %collective-permute-done = bf16[88,2048]{1,0:T(8,128)(2,1)S(1)} collective-permute-done((bf16[88,2048]{1,0:T(8,128)(2,1)S(1)}, bf16[88,2048]{1,0:T(8,128)(2,1)S(1)}, u32[]{:S(2)}, u32[]{:S(2)}) %collective-permute-start) | collective-permute-done | bytes 360480 | tf_op jit(solution)/shard_map/ppermute | solution.py:457
  3.0 2.1 %maximum_select_fusion.piece = bf16[176,2048]{1,0:T(8,128)(2,1)} fusion(bf16[88,2048]{1,0:T(8,128)(2,1)S(1)} %collective-permute-done, bf16[88,2048]{1,0:T(8,128)(2,1)} %bitcast.17, bf16[88,2048]{1,0:T(8,128)(2,1)} %bitcast.16, pred[]{:T(512)S(6)} %eq.5), kind=kLoop, calls=%fused_computation | loop fusion | flops 3244032 | bytes 1802241 | tf_op jit(solution)/shard_map/jit(_where)/select_n | solution.py:458
  5.1 117.8 %shard_map.91 = bf16[16,176,256]{2,1,0:T(8,128)(2,1)} custom-call(bf16[256,2048]{1,0:T(8,128)(2,1)} %bitcast.18, bf16[256,2048]{1,0:T(8,128)(2,1)} %bitcast.19, bf16[256,128]{1,0:T(8,128)(2,1)} %bitcast.21, bf16[256,128]{1,0:T(8,128)(2,1)} %bitcast.22, f32[32,256]{1,0:T(8,128)} %bitcast.23, f32[12,32,256]{2,1,0:T(8,128)} %bitcast.20, f32[1,2048]{1,0:T(1,128)} %bitcast.24, ...), custom_call_target="tpu_custom_call" | custom-call | flops 5905580032 | bytes 23068672 | tf_op jit(solution)/shard_map/pallas_call | solution.py:469
  122.8 2.5 %copy.10 = bf16[2816,256]{0,1:T(8,128)(2,1)} copy(bf16[2816,256]{1,0:T(8,128)(2,1)} %bitcast.15) | data formatting | bytes 2883584 | tf_op jit(solution)/shard_map/reshape | solution.py:509
Async XLA Ops:
  1.1 1.8 %collective-permute-start = (bf16[88,2048]{1,0:T(8,128)(2,1)S(1)}, bf16[88,2048]{1,0:T(8,128)(2,1)S(1)}, u32[]{:S(2)}, u32[]{:S(2)}) collective-permute-start(bf16[88,2048]{1,0:T(8,128)(2,1)S(1)} %broadcast_select_fusion), channel_id=1, source_target_pairs={{0,1},{1,0},{2,3},{3,2},{4,5},{5,4},{6,7},{7,6},{8,9},{9,8},{10,11... | collective-permute-start | bytes 1081352 | tf_op jit(solution)/shard_map/ppermute | solution.py:457
